TPU v7x, 32 devices: a whole 2x2x4 slice. The times are simulated.
32 devices in a mesh: gx: 4 (over z), gy: 2 (over y), gz: 4 (over x, core).
Axes of the slice: x: 2, y: 2, z: 4, core: 2. Of those that a mesh axis runs over, the one named last changes fastest.
Arguments:
- fluid_velocity: float32 [3, 16, 16, 1024], P(None, 'gx', 'gy', 'gz'), may hold values from -6 to 6
- particle_velocity: float32 [2048, 3, 128], P(('gx', 'gy', 'gz')), may hold values from -4 to 4
- diameter: float32 [2048, 128], P(('gx', 'gy', 'gz')), may hold values from 0.4 to 0.7
- particle_cell: int32 [2048, 128], P(('gx', 'gy', 'gz')), may hold values from 0 to 8191
- block_owner: int32 [2048, 1], P(('gx', 'gy', 'gz')), may hold values from 0 to 7; in each aligned block of 64 rows (0 to 63, 64 to 127, ...) at most 32 rows name the same one
Outputs:
- particle_accel: float32 [2048, 3, 128], P(('gx', 'gy', 'gz'))
- voidage: float32 [16, 16, 1024], P('gx', 'gy', 'gz')
- fluid_next: float32 [3, 16, 16, 1024], P(None, 'gx', 'gy', 'gz')
Inputs may be any that keep to these rules, and one draw needn't show every extreme that they name: `block_owner`: among the 64 blocks of one device at most 32 name one owner, and in every draw some device has exactly 32 blocks for some owner. An owner is a device of the same gz plane, numbered gx * 2 + gy. `particle_cell`: A cell of the owner's brick, numbered (x * 8 + y) * 256 + z in the brick's own coordinates.
All inputs are finite; a program needn't handle non-finite values.
Results may differ from a plain program's by a relative error of at most 0.00012.
Values sent between devices are 32-bit elements; how exact they have to be, the bound alone decides.
A program may use at most 128 MiB of HBM per device.

v0:
```python
import math

import jax
import jax.numpy as jnp
from jax import lax
from jax.sharding import PartitionSpec as P

VISCOSITY = 0.1
FLUID_DENSITY = 0.05
SOLID_DENSITY = 2.5
TIME_STEP = 0.05
VOID_FLOOR = 0.35
SPREAD = 0.1
HIGH = lax.Precision.HIGHEST


def extended(cells, sides, width):
    for axis, dim in sides:
        count = lax.axis_size(axis)
        ends = count - 1
        head = lax.slice_in_dim(cells, 0, width, axis=dim)
        tail = lax.slice_in_dim(cells, cells.shape[dim] - width, cells.shape[dim], axis=dim)
        cells = jnp.concatenate(
            [
                lax.ppermute(tail, axis, [(i, (i + 1) % count) for i in range(ends)]),
                cells,
                lax.ppermute(head, axis, [((i + 1) % count, i) for i in range(ends)]),
            ],
            axis=dim,
        )
    return cells


def neighbours(padded):
    total = padded[..., 2:, 1:-1, 1:-1] + padded[..., :-2, 1:-1, 1:-1]
    total = total + padded[..., 1:-1, 2:, 1:-1] + padded[..., 1:-1, :-2, 1:-1]
    return total + padded[..., 1:-1, 1:-1, 2:] + padded[..., 1:-1, 1:-1, :-2]


def drag_force(slip, diam_part, void_at):
    slip_speed = jnp.sqrt(jnp.sum(slip * slip, axis=1))
    reynolds = jnp.maximum(void_at * diam_part * slip_speed / VISCOSITY, 1.0)
    drag_coeff = (0.63 + 4.8 / jnp.sqrt(reynolds)) ** 2
    chi_exp = 3.7 - 0.65 * jnp.exp(-0.5 * (1.5 - jnp.log10(reynolds)) ** 2)
    magnitude = 0.5 * drag_coeff * FLUID_DENSITY * (math.pi / 4) * diam_part * diam_part
    magnitude = magnitude * jnp.exp((2.0 - chi_exp) * jnp.log(void_at)) * slip_speed
    return magnitude[:, None, :] * slip


def block_rows(total):
    return math.gcd(total, 8192)


def lookup_cells(table, cells, lane_count):
    comps = table.shape[0]
    plane_count = table.shape[1] // lane_count
    grid = (
        table.reshape(comps, plane_count, lane_count)
        .transpose(1, 0, 2)
        .reshape(plane_count, comps * lane_count)
    )
    flat = cells.reshape(-1)
    rows = block_rows(flat.shape[0])
    blocked = flat.reshape(-1, rows)

    def one_block(cell_rows):
        plane_hot = (
            cell_rows[:, None] // lane_count == jnp.arange(plane_count, dtype=jnp.int32)[None, :]
        ).astype(jnp.float32)
        lane_hot = (
            cell_rows[:, None] % lane_count == jnp.arange(lane_count, dtype=jnp.int32)[None, :]
        ).astype(jnp.float32)
        picked = jnp.dot(plane_hot, grid, precision=HIGH, preferred_element_type=jnp.float32)
        picked = picked.reshape(rows, comps, lane_count)
        return jnp.sum(picked * lane_hot[:, None, :], axis=2)

    result = lax.map(one_block, blocked).reshape(-1, comps)
    return jnp.moveaxis(result, 1, 0).reshape((comps,) + cells.shape)


def deposit_cells(values, cells, cell_count, lane_count):
    comps = values.shape[0]
    plane_count = cell_count // lane_count
    flat = cells.reshape(-1)
    rows = block_rows(flat.shape[0])
    blocked = flat.reshape(-1, rows)
    blocked_values = jnp.moveaxis(values.reshape(comps, -1, rows), 0, 1)

    def add_block(total, pieces):
        cell_rows, value_rows = pieces
        plane_hot = (
            cell_rows[:, None] // lane_count == jnp.arange(plane_count, dtype=jnp.int32)[None, :]
        ).astype(jnp.float32)
        lane_hot = (
            cell_rows[:, None] % lane_count == jnp.arange(lane_count, dtype=jnp.int32)[None, :]
        ).astype(jnp.float32)
        spread_rows = (value_rows.T[:, :, None] * lane_hot[:, None, :]).reshape(
            rows, comps * lane_count
        )
        return (
            total
            + jnp.dot(plane_hot.T, spread_rows, precision=HIGH, preferred_element_type=jnp.float32),
            None,
        )

    start = jnp.zeros((plane_count, comps * lane_count), jnp.float32)
    total, unused = lax.scan(add_block, start, (blocked, blocked_values))
    return (
        total.reshape(plane_count, comps, lane_count).transpose(1, 0, 2).reshape(comps, cell_count)
    )


def move_particles(send_float, send_cells):
    got_float, got_cells = (
        lax.all_to_all(send_float, ("gx", "gy"), split_axis=0, concat_axis=0, tiled=True),
        lax.all_to_all(send_cells, ("gx", "gy"), split_axis=0, concat_axis=0, tiled=True),
    )
    return (got_float, got_cells)


def move_values(values):
    return lax.all_to_all(values, ("gx", "gy"), split_axis=0, concat_axis=0, tiled=True)


def per_device(fluid_velocity, particle_velocity, diameter, particle_cell, block_owner):
    owners = lax.axis_size("gx") * lax.axis_size("gy")
    blk_count, per_block = diameter.shape
    capacity = 4 * blk_count // owners
    slot_count = owners * capacity
    cell_shape = fluid_velocity.shape[1:]
    lane_count = cell_shape[2]
    cell_count = cell_shape[0] * cell_shape[1] * cell_shape[2]
    velocity_pad = extended(fluid_velocity, (("gx", 1), ("gy", 2), ("gz", 3)), 1)
    block_dest = block_owner[:, 0]
    matches = (block_dest[:, None] == jnp.arange(owners, dtype=jnp.int32)[None, :]).astype(
        jnp.int32
    )
    earlier = jnp.cumsum(matches, axis=0) - matches
    slot_rank = jnp.sum(earlier * matches, axis=1)
    position = block_dest * capacity + slot_rank
    placing = (jnp.arange(slot_count, dtype=jnp.int32)[:, None] == position[None, :]).astype(
        jnp.float32
    )
    payload = jnp.concatenate(
        [particle_velocity, diameter[:, None, :], particle_cell.astype(jnp.float32)[:, None, :]],
        axis=1,
    )
    placed = jnp.einsum(
        "sb,bcp->scp", placing, payload, precision=HIGH, preferred_element_type=jnp.float32
    )
    send_float = placed[:, :4]
    send_cells = placed[:, 4].astype(jnp.int32)
    got_float, got_cells = move_particles(send_float, send_cells)
    got_diam = got_float[:, 3]
    got_volume = math.pi / 6 * got_diam * got_diam * got_diam
    solid = deposit_cells(got_volume[None], got_cells, cell_count, lane_count)[0].reshape(
        cell_shape
    )
    solid_pad = extended(solid, (("gx", 0), ("gy", 1), ("gz", 2)), 1)
    smooth = (solid + SPREAD * neighbours(solid_pad)) / (1.0 + 6 * SPREAD)
    voidage = jnp.maximum(1.0 - smooth, VOID_FLOOR)
    table = jnp.concatenate(
        [fluid_velocity.reshape(3, cell_count), voidage.reshape(1, cell_count)], axis=0
    )
    looked = jnp.moveaxis(lookup_cells(table, got_cells, lane_count), 0, 1)
    deposit_force = drag_force(looked[:, :3] - got_float[:, :3], got_diam, looked[:, 3])
    returned = move_values(deposit_force)
    own_force = jnp.einsum(
        "sb,scp->bcp", placing, returned, precision=HIGH, preferred_element_type=jnp.float32
    )
    own_volume = math.pi / 6 * diameter * diameter * diameter
    particle_accel = own_force / (SOLID_DENSITY * own_volume)[:, None, :]
    source = -deposit_cells(jnp.moveaxis(deposit_force, 1, 0), got_cells, cell_count, lane_count)
    source = source.reshape((3,) + cell_shape)
    laplace = neighbours(velocity_pad) - 6.0 * fluid_velocity
    fluid_next = fluid_velocity + TIME_STEP * (laplace + source / (FLUID_DENSITY * voidage)[None])
    return (particle_accel, voidage, fluid_next)


def solution(mesh):
    placed = (
        P(None, "gx", "gy", "gz"),
        P(("gx", "gy", "gz"), None, None),
        P(("gx", "gy", "gz"), None),
        P(("gx", "gy", "gz"), None),
        P(("gx", "gy", "gz"), None),
    )
    return jax.shard_map(
        per_device,
        mesh=mesh,
        in_specs=placed,
        out_specs=(
            P(("gx", "gy", "gz"), None, None),
            P("gx", "gy", "gz"),
            P(None, "gx", "gy", "gz"),
        ),
        check_vma=False,
    )
```

profile of v0, /device:TPU:0, one launch (start us, length us, event | category | flops | bytes accessed | tf_op | source)
XLA Modules:
  0.0 258.3 jit_solution(8986820296241873944)
XLA Ops:
  0.6 0.7 fusion.58
  1.5 0.8 select_reduce_fusion
  2.3 0.7 multiply_add_fusion
  3.0 0.8 convert_bitcast_fusion
  3.7 1.4 fusion.22
  5.2 0.7 slice_convert_fusion
  5.8 7.3 %all-to-all-start = ((s32[8,32,128]{2,1,0:T(8,128)}), s32[8,32,128]{2,1,0:T(8,128)S(1)}, u32[]{:S(2)}, u32[]{:S(2)}) async-start(s32[8,32,128]{2,1,0:T(8,128)} %bitcast.7), calls=%async_computation | async-start | bytes 262144 | tf_op jit(solution)/shard_map/all_to_all | solution.py:116
  13.2 1.1 copy.66
  14.3 6.2 %all-to-all-done = s32[8,32,128]{2,1,0:T(8,128)S(1)} async-done(((s32[8,32,128]{2,1,0:T(8,128)}), s32[8,32,128]{2,1,0:T(8,128)S(1)}, u32[]{:S(2)}, u32[]{:S(2)}) %all-to-all-start) | async-done | bytes 131104 | tf_op jit(solution)/shard_map/all_to_all | solution.py:116
  20.5 3.5 %all-to-all-start.1 = ((f32[256,4,128]{2,1,0:T(4,128)}), f32[256,4,128]{2,1,0:T(4,128)S(1)}, u32[]{:S(2)}, u32[]{:S(2)}) async-start(f32[256,4,128]{2,1,0:T(4,128)} %copy.66), calls=%async_computation.1 | async-start | bytes 1048576 | tf_op jit(solution)/shard_map/all_to_all | solution.py:115
  24.0 0.8 fusion.63
  24.7 3.8 %collective-permute-start.7 = (f32[3,1,8,256]{3,2,1,0:T(8,128)S(1)}, f32[3,1,8,256]{3,2,1,0:T(8,128)S(1)}, u32[]{:S(2)}, u32[]{:S(2)}) collective-permute-start(f32[3,1,8,256]{3,2,1,0:T(8,128)S(1)} %get-tuple-element.241), channel_id=1, source_target_pairs={{0,8},{8,16},{16,24},{1,9},{9,17},{17,25},{2,10},{10,18},{18,26},{... | collective-permute-start | bytes 73736 | tf_op jit(solution)/shard_map/ppermute | solution.py:25
  28.6 1.3 collective-permute-start.6
  29.9 0.8 fusion.45
  30.6 1.0 copy.71
  31.6 0.3 collective-permute-done.7
  31.9 0.9 constant_dynamic-update-slice_fusion.1
  32.8 1.7 collective-permute-done.6
  34.6 1.3 collective-permute-start.8
  35.9 4.5 %collective-permute-start.9 = (f32[3,6,1,256]{3,2,1,0:T(1,128)S(1)}, f32[3,6,1,256]{3,2,1,0:T(1,128)S(1)}, u32[]{:S(2)}, u32[]{:S(2)}) collective-permute-start(f32[3,6,1,256]{3,2,1,0:T(1,128)S(1)} %get-tuple-element.238), channel_id=1, source_target_pairs={{0,4},{1,5},{2,6},{3,7},{8,12},{9,13},{10,14},{11,15},{16,20},{17,... | collective-permute-start | bytes 55304 | tf_op jit(solution)/shard_map/ppermute | solution.py:25
  40.8 16.0 %while.39 = (s32[]{:T(128)}, f32[32,256]{1,0:T(8,128)S(1)}, s32[4,8192]{1,0:T(4,128)S(1)}, f32[4,1,8192]{2,1,0:T(1,128)S(1)}, s32[]{:T(128)}, /*index=5*/s32[]{:T(128)}) while((s32[]{:T(128)}, f32[32,256]{1,0:T(8,128)S(1)}, s32[4,8192]{1,0:T(4,128)S(1)}, f32[4,1,8192]{2,1,0:T(1,128)S(1)}, s32[]{:T(128)}, /*index=5*/s32[]{:T(128)}) %tuple.96), condition=%wide.region_3.4_spmd.clone, body=%wide.region_2.3_spmd.clone.sunk | while | flops 809934848 | bytes 393303 | solution.py:107
  40.9 3.9 %fusion.76 = f32[32,256]{1,0:T(8,128)S(1)} fusion(f32[8192]{0:T(1024)S(1)} %bitcast.104, s32[8192]{0:T(1024)S(1)} %get-tuple-element.327, s32[8192]{0:T(1024)S(1)} %get-tuple-element.328, f32[32,256]{1,0:T(8,128)S(1)} %get-tuple-element.342, pred[]{:T(512)S(6)} %compare.48), kind=kOutput, calls=%fused_computation.22.clone.1 | convolution fusion | flops 809779200 | bytes 163841 | tf_op jit(solution)/shard_map/while/body/eval_jaxpr/dot_general | solution.py:102
  44.9 3.9 %fusion.76 = f32[32,256]{1,0:T(8,128)S(1)} fusion(f32[8192]{0:T(1024)S(1)} %bitcast.104, s32[8192]{0:T(1024)S(1)} %get-tuple-element.327, s32[8192]{0:T(1024)S(1)} %get-tuple-element.328, f32[32,256]{1,0:T(8,128)S(1)} %get-tuple-element.342, pred[]{:T(512)S(6)} %compare.48), kind=kOutput, calls=%fused_computation.22.clone.1 | convolution fusion | flops 809779200 | bytes 163841 | tf_op jit(solution)/shard_map/while/body/eval_jaxpr/dot_general | solution.py:102
  48.9 3.9 %fusion.76 = f32[32,256]{1,0:T(8,128)S(1)} fusion(f32[8192]{0:T(1024)S(1)} %bitcast.104, s32[8192]{0:T(1024)S(1)} %get-tuple-element.327, s32[8192]{0:T(1024)S(1)} %get-tuple-element.328, f32[32,256]{1,0:T(8,128)S(1)} %get-tuple-element.342, pred[]{:T(512)S(6)} %compare.48), kind=kOutput, calls=%fused_computation.22.clone.1 | convolution fusion | flops 809779200 | bytes 163841 | tf_op jit(solution)/shard_map/while/body/eval_jaxpr/dot_general | solution.py:102
  53.0 3.9 %fusion.76 = f32[32,256]{1,0:T(8,128)S(1)} fusion(f32[8192]{0:T(1024)S(1)} %bitcast.104, s32[8192]{0:T(1024)S(1)} %get-tuple-element.327, s32[8192]{0:T(1024)S(1)} %get-tuple-element.328, f32[32,256]{1,0:T(8,128)S(1)} %get-tuple-element.342, pred[]{:T(512)S(6)} %compare.48), kind=kOutput, calls=%fused_computation.22.clone.1 | convolution fusion | flops 809779200 | bytes 163841 | tf_op jit(solution)/shard_map/while/body/eval_jaxpr/dot_general | solution.py:102
  56.9 1.3 collective-permute-start
  58.2 6.3 %collective-permute-start.1 = (f32[1,8,256]{2,1,0:T(8,128)S(1)}, f32[1,8,256]{2,1,0:T(8,128)S(1)}, u32[]{:S(2)}, u32[]{:S(2)}) collective-permute-start(f32[1,8,256]{2,1,0:T(8,128)S(1)} %get-tuple-element.246), channel_id=1, source_target_pairs={{0,8},{8,16},{16,24},{1,9},{9,17},{17,25},{2,10},{10,18},{18,26},{... | collective-permute-start | bytes 24584 | tf_op jit(solution)/shard_map/ppermute | solution.py:25
  64.6 1.3 collective-permute-done.1
  65.8 1.3 collective-permute-start.2
  67.1 4.5 %collective-permute-start.3 = (f32[6,1,256]{2,1,0:T(1,128)S(1)}, f32[6,1,256]{2,1,0:T(1,128)S(1)}, u32[]{:S(2)}, u32[]{:S(2)}) collective-permute-start(f32[6,1,256]{2,1,0:T(1,128)S(1)} %get-tuple-element.244), channel_id=1, source_target_pairs={{0,4},{1,5},{2,6},{3,7},{8,12},{9,13},{10,14},{11,15},{16,20},{17,... | collective-permute-start | bytes 18440 | tf_op jit(solution)/shard_map/ppermute | solution.py:25
  71.8 1.2 collective-permute-done.3
  73.1 1.3 collective-permute-start.4
  74.4 3.0 %collective-permute-start.5 = (f32[6,10,1]{2,1,0:T(8,128)S(1)}, f32[6,10,1]{2,1,0:T(8,128)S(1)}, u32[]{:S(2)}, u32[]{:S(2)}) collective-permute-start(f32[6,10,1]{2,1,0:T(8,128)S(1)} %get-tuple-element.243), channel_id=1, source_target_pairs={{0,1},{1,2},{2,3},{4,5},{5,6},{6,7},{8,9},{9,10},{10,11},{12,13},{... | collective-permute-start | bytes 728 | tf_op jit(solution)/shard_map/ppermute | solution.py:25
  77.4 1.3 collective-permute-start.10
  78.7 3.8 %collective-permute-start.11 = (f32[3,6,10,1]{3,2,1,0:T(8,128)S(1)}, f32[3,6,10,1]{3,2,1,0:T(8,128)S(1)}, u32[]{:S(2)}, u32[]{:S(2)}) collective-permute-start(f32[3,6,10,1]{3,2,1,0:T(8,128)S(1)} %get-tuple-element.237), channel_id=1, source_target_pairs={{0,1},{1,2},{2,3},{4,5},{5,6},{6,7},{8,9},{9,10},{10,11},{12,13},{... | collective-permute-start | bytes 2168 | tf_op jit(solution)/shard_map/ppermute | solution.py:25
  82.9 0.5 copy-done.1
  83.3 63.5 %while.38 = (s32[]{:T(128)}, f32[4,8192,4]{1,2,0:T(4,128)S(1)}, s32[4,8192]{1,0:T(4,128)S(1)}, f32[32,1024]{1,0:T(8,128)S(1)}, s32[]{:T(128)}) while((s32[]{:T(128)}, f32[4,8192,4]{1,2,0:T(4,128)S(1)}, s32[4,8192]{1,0:T(4,128)S(1)}, f32[32,1024]{1,0:T(8,128)S(1)}, s32[]{:T(128)}) %tuple.106), condition=%wide.region_6.7_spmd, body=%wide.region_4.6_spmd.sunk | while | flops 3242582016 | bytes 17530948 | solution.py:77
  83.4 1.0 fusion.74
  84.4 14.8 %multiply_reduce_fusion.3 = f32[8192,4]{0,1:T(4,128)S(1)} fusion(f32[8192,256]{0,1:T(8,128)S(1)} %fusion.74, f32[32,1024]{1,0:T(8,128)S(1)} %get-tuple-element.366, s32[8192]{0:T(1024)S(1)} %get-tuple-element.322), kind=kOutput, calls=%fused_computation.clone.1 | convolution fusion | flops 3238232064 | bytes 8683520 | tf_op jit(solution)/shard_map/while/body/eval_jaxpr/dot_general | solution.py:73
  99.3 1.0 fusion.74
  100.3 14.8 %multiply_reduce_fusion.3 = f32[8192,4]{0,1:T(4,128)S(1)} fusion(f32[8192,256]{0,1:T(8,128)S(1)} %fusion.74, f32[32,1024]{1,0:T(8,128)S(1)} %get-tuple-element.366, s32[8192]{0:T(1024)S(1)} %get-tuple-element.322), kind=kOutput, calls=%fused_computation.clone.1 | convolution fusion | flops 3238232064 | bytes 8683520 | tf_op jit(solution)/shard_map/while/body/eval_jaxpr/dot_general | solution.py:73
  115.2 1.0 fusion.74
  116.2 14.8 %multiply_reduce_fusion.3 = f32[8192,4]{0,1:T(4,128)S(1)} fusion(f32[8192,256]{0,1:T(8,128)S(1)} %fusion.74, f32[32,1024]{1,0:T(8,128)S(1)} %get-tuple-element.366, s32[8192]{0:T(1024)S(1)} %get-tuple-element.322), kind=kOutput, calls=%fused_computation.clone.1 | convolution fusion | flops 3238232064 | bytes 8683520 | tf_op jit(solution)/shard_map/while/body/eval_jaxpr/dot_general | solution.py:73
  131.1 1.0 fusion.74
  132.0 14.8 %multiply_reduce_fusion.3 = f32[8192,4]{0,1:T(4,128)S(1)} fusion(f32[8192,256]{0,1:T(8,128)S(1)} %fusion.74, f32[32,1024]{1,0:T(8,128)S(1)} %get-tuple-element.366, s32[8192]{0:T(1024)S(1)} %get-tuple-element.322), kind=kOutput, calls=%fused_computation.clone.1 | convolution fusion | flops 3238232064 | bytes 8683520 | tf_op jit(solution)/shard_map/while/body/eval_jaxpr/dot_general | solution.py:73
  147.0 0.2 fusion.30
  147.2 1.1 copy.74
  148.5 0.3 copy.95
  148.8 7.4 %all-to-all-start.2 = ((f32[256,3,128]{2,1,0:T(4,128)}), f32[256,3,128]{2,1,0:T(4,128)S(1)}, u32[]{:S(2)}, u32[]{:S(2)}) async-start(f32[256,3,128]{2,1,0:T(4,128)} %copy.74), calls=%async_computation.2 | async-start | bytes 1048576 | tf_op jit(solution)/shard_map/all_to_all | solution.py:122
  156.2 100.2 %while.40 = (s32[]{:T(128)}, f32[32,768]{1,0:T(8,128)S(1)}, s32[4,8192]{1,0:T(4,128)S(1)}, f32[4,3,8192]{2,1,0:T(4,128)S(1)}, s32[]{:T(128)}, /*index=5*/s32[]{:T(128)}) while((s32[]{:T(128)}, f32[32,768]{1,0:T(8,128)S(1)}, s32[4,8192]{1,0:T(4,128)S(1)}, f32[4,3,8192]{2,1,0:T(4,128)S(1)}, s32[]{:T(128)}, ...), condition=%wide.region_9.10_spmd.clone, body=%wide.region_8.9_spmd.clone.sunk | while | flops 2426871808 | bytes 67829848 | solution.py:107
  156.3 1.0 fusion.78
  157.3 8.5 %broadcast_multiply_fusion.4 = f32[8192,3,256]{0,2,1:T(8,128)} fusion(f32[8192,256]{0,1:T(8,128)S(1)} %fusion.78, f32[8192,3]{0,1:T(4,128)S(1)} %dynamic-slice_bitcast_fusion.2), kind=kLoop, calls=%fused_computation.36.clone.1 | loop fusion | flops 6291456 | bytes 33652736 | tf_op jit(solution)/shard_map/while/body/eval_jaxpr/mul | solution.py:97
  165.8 15.4 %convolution_add_fusion.2 = f32[32,768]{1,0:T(8,128)S(1)} fusion(f32[8192,768]{0,1:T(8,128)} %bitcast.89, s32[8192]{0:T(1024)S(1)} %get-tuple-element.334, f32[32,768]{1,0:T(8,128)S(1)} %get-tuple-element.375, pred[]{:T(512)S(6)} %compare.49), kind=kOutput, calls=%fused_computation.39.clone.1 | convolution fusion | flops 2416230400 | bytes 25395200 | tf_op jit(solution)/shard_map/while/body/eval_jaxpr/dot_general | solution.py:102
  181.3 1.0 fusion.78
  182.3 8.5 %broadcast_multiply_fusion.4 = f32[8192,3,256]{0,2,1:T(8,128)} fusion(f32[8192,256]{0,1:T(8,128)S(1)} %fusion.78, f32[8192,3]{0,1:T(4,128)S(1)} %dynamic-slice_bitcast_fusion.2), kind=kLoop, calls=%fused_computation.36.clone.1 | loop fusion | flops 6291456 | bytes 33652736 | tf_op jit(solution)/shard_map/while/body/eval_jaxpr/mul | solution.py:97
  190.8 15.4 %convolution_add_fusion.2 = f32[32,768]{1,0:T(8,128)S(1)} fusion(f32[8192,768]{0,1:T(8,128)} %bitcast.89, s32[8192]{0:T(1024)S(1)} %get-tuple-element.334, f32[32,768]{1,0:T(8,128)S(1)} %get-tuple-element.375, pred[]{:T(512)S(6)} %compare.49), kind=kOutput, calls=%fused_computation.39.clone.1 | convolution fusion | flops 2416230400 | bytes 25395200 | tf_op jit(solution)/shard_map/while/body/eval_jaxpr/dot_general | solution.py:102
  206.4 1.0 fusion.78
  207.4 8.5 %broadcast_multiply_fusion.4 = f32[8192,3,256]{0,2,1:T(8,128)} fusion(f32[8192,256]{0,1:T(8,128)S(1)} %fusion.78, f32[8192,3]{0,1:T(4,128)S(1)} %dynamic-slice_bitcast_fusion.2), kind=kLoop, calls=%fused_computation.36.clone.1 | loop fusion | flops 6291456 | bytes 33652736 | tf_op jit(solution)/shard_map/while/body/eval_jaxpr/mul | solution.py:97
  215.9 15.4 %convolution_add_fusion.2 = f32[32,768]{1,0:T(8,128)S(1)} fusion(f32[8192,768]{0,1:T(8,128)} %bitcast.89, s32[8192]{0:T(1024)S(1)} %get-tuple-element.334, f32[32,768]{1,0:T(8,128)S(1)} %get-tuple-element.375, pred[]{:T(512)S(6)} %compare.49), kind=kOutput, calls=%fused_computation.39.clone.1 | convolution fusion | flops 2416230400 | bytes 25395200 | tf_op jit(solution)/shard_map/while/body/eval_jaxpr/dot_general | solution.py:102
  231.4 1.0 fusion.78
  232.5 8.5 %broadcast_multiply_fusion.4 = f32[8192,3,256]{0,2,1:T(8,128)} fusion(f32[8192,256]{0,1:T(8,128)S(1)} %fusion.78, f32[8192,3]{0,1:T(4,128)S(1)} %dynamic-slice_bitcast_fusion.2), kind=kLoop, calls=%fused_computation.36.clone.1 | loop fusion | flops 6291456 | bytes 33652736 | tf_op jit(solution)/shard_map/while/body/eval_jaxpr/mul | solution.py:97
  241.0 15.4 %convolution_add_fusion.2 = f32[32,768]{1,0:T(8,128)S(1)} fusion(f32[8192,768]{0,1:T(8,128)} %bitcast.89, s32[8192]{0:T(1024)S(1)} %get-tuple-element.334, f32[32,768]{1,0:T(8,128)S(1)} %get-tuple-element.375, pred[]{:T(512)S(6)} %compare.49), kind=kOutput, calls=%fused_computation.39.clone.1 | convolution fusion | flops 2416230400 | bytes 25395200 | tf_op jit(solution)/shard_map/while/body/eval_jaxpr/dot_general | solution.py:102
  256.5 0.8 fusion.37
  257.4 0.9 convolution_divide_fusion
  (76 shorter events, 2.4 us)
Async XLA Ops:
  5.8 14.6 %all-to-all-start = ((s32[8,32,128]{2,1,0:T(8,128)}), s32[8,32,128]{2,1,0:T(8,128)S(1)}, u32[]{:S(2)}, u32[]{:S(2)}) async-start(s32[8,32,128]{2,1,0:T(8,128)} %bitcast.7), calls=%async_computation | async-start | bytes 262144 | tf_op jit(solution)/shard_map/all_to_all | solution.py:116
  20.5 20.0 %all-to-all-start.1 = ((f32[256,4,128]{2,1,0:T(4,128)}), f32[256,4,128]{2,1,0:T(4,128)S(1)}, u32[]{:S(2)}, u32[]{:S(2)}) async-start(f32[256,4,128]{2,1,0:T(4,128)} %copy.66), calls=%async_computation.1 | async-start | bytes 1048576 | tf_op jit(solution)/shard_map/all_to_all | solution.py:115
  24.7 7.2 %collective-permute-start.7 = (f32[3,1,8,256]{3,2,1,0:T(8,128)S(1)}, f32[3,1,8,256]{3,2,1,0:T(8,128)S(1)}, u32[]{:S(2)}, u32[]{:S(2)}) collective-permute-start(f32[3,1,8,256]{3,2,1,0:T(8,128)S(1)} %get-tuple-element.241), channel_id=1, source_target_pairs={{0,8},{8,16},{16,24},{1,9},{9,17},{17,25},{2,10},{10,18},{18,26},{... | collective-permute-start | bytes 73736 | tf_op jit(solution)/shard_map/ppermute | solution.py:25
  28.6 6.0 %collective-permute-start.6 = (f32[3,1,8,256]{3,2,1,0:T(8,128)S(1)}, f32[3,1,8,256]{3,2,1,0:T(8,128)S(1)}, u32[]{:S(2)}, u32[]{:S(2)}) collective-permute-start(f32[3,1,8,256]{3,2,1,0:T(8,128)S(1)} %get-tuple-element.240), channel_id=1, source_target_pairs={{8,0},{16,8},{24,16},{9,1},{17,9},{25,17},{10,2},{18,10},{26,18},{... | collective-permute-start | bytes 73736 | tf_op jit(solution)/shard_map/ppermute | solution.py:27
  34.6 29.9 %collective-permute-start.8 = (f32[3,6,1,256]{3,2,1,0:T(1,128)S(1)}, f32[3,6,1,256]{3,2,1,0:T(1,128)S(1)}, u32[]{:S(2)}, u32[]{:S(2)}) collective-permute-start(f32[3,6,1,256]{3,2,1,0:T(1,128)S(1)} %get-tuple-element.239), channel_id=1, source_target_pairs={{4,0},{5,1},{6,2},{7,3},{12,8},{13,9},{14,10},{15,11},{20,16},{21,... | collective-permute-start | bytes 55304 | tf_op jit(solution)/shard_map/ppermute | solution.py:27
  35.9 28.6 %collective-permute-start.9 = (f32[3,6,1,256]{3,2,1,0:T(1,128)S(1)}, f32[3,6,1,256]{3,2,1,0:T(1,128)S(1)}, u32[]{:S(2)}, u32[]{:S(2)}) collective-permute-start(f32[3,6,1,256]{3,2,1,0:T(1,128)S(1)} %get-tuple-element.238), channel_id=1, source_target_pairs={{0,4},{1,5},{2,6},{3,7},{8,12},{9,13},{10,14},{11,15},{16,20},{17,... | collective-permute-start | bytes 55304 | tf_op jit(solution)/shard_map/ppermute | solution.py:25
  56.9 7.7 %collective-permute-start = (f32[1,8,256]{2,1,0:T(8,128)S(1)}, f32[1,8,256]{2,1,0:T(8,128)S(1)}, u32[]{:S(2)}, u32[]{:S(2)}) collective-permute-start(f32[1,8,256]{2,1,0:T(8,128)S(1)} %get-tuple-element.247), channel_id=1, source_target_pairs={{8,0},{16,8},{24,16},{9,1},{17,9},{25,17},{10,2},{18,10},{26,18},{... | collective-permute-start | bytes 24584 | tf_op jit(solution)/shard_map/ppermute | solution.py:27
  58.2 7.7 %collective-permute-start.1 = (f32[1,8,256]{2,1,0:T(8,128)S(1)}, f32[1,8,256]{2,1,0:T(8,128)S(1)}, u32[]{:S(2)}, u32[]{:S(2)}) collective-permute-start(f32[1,8,256]{2,1,0:T(8,128)S(1)} %get-tuple-element.246), channel_id=1, source_target_pairs={{0,8},{8,16},{16,24},{1,9},{9,17},{17,25},{2,10},{10,18},{18,26},{... | collective-permute-start | bytes 24584 | tf_op jit(solution)/shard_map/ppermute | solution.py:25
  65.8 6.0 %collective-permute-start.2 = (f32[6,1,256]{2,1,0:T(1,128)S(1)}, f32[6,1,256]{2,1,0:T(1,128)S(1)}, u32[]{:S(2)}, u32[]{:S(2)}) collective-permute-start(f32[6,1,256]{2,1,0:T(1,128)S(1)} %get-tuple-element.245), channel_id=1, source_target_pairs={{4,0},{5,1},{6,2},{7,3},{12,8},{13,9},{14,10},{15,11},{20,16},{21,... | collective-permute-start | bytes 18440 | tf_op jit(solution)/shard_map/ppermute | solution.py:27
  67.1 5.9 %collective-permute-start.3 = (f32[6,1,256]{2,1,0:T(1,128)S(1)}, f32[6,1,256]{2,1,0:T(1,128)S(1)}, u32[]{:S(2)}, u32[]{:S(2)}) collective-permute-start(f32[6,1,256]{2,1,0:T(1,128)S(1)} %get-tuple-element.244), channel_id=1, source_target_pairs={{0,4},{1,5},{2,6},{3,7},{8,12},{9,13},{10,14},{11,15},{16,20},{17,... | collective-permute-start | bytes 18440 | tf_op jit(solution)/shard_map/ppermute | solution.py:25
  73.1 9.5 %collective-permute-start.4 = (f32[6,10,1]{2,1,0:T(8,128)S(1)}, f32[6,10,1]{2,1,0:T(8,128)S(1)}, u32[]{:S(2)}, u32[]{:S(2)}) collective-permute-start(f32[6,10,1]{2,1,0:T(8,128)S(1)} %get-tuple-element.242), channel_id=1, source_target_pairs={{1,0},{2,1},{3,2},{5,4},{6,5},{7,6},{9,8},{10,9},{11,10},{13,12},{... | collective-permute-start | bytes 728 | tf_op jit(solution)/shard_map/ppermute | solution.py:27
  74.4 8.2 %collective-permute-start.5 = (f32[6,10,1]{2,1,0:T(8,128)S(1)}, f32[6,10,1]{2,1,0:T(8,128)S(1)}, u32[]{:S(2)}, u32[]{:S(2)}) collective-permute-start(f32[6,10,1]{2,1,0:T(8,128)S(1)} %get-tuple-element.243), channel_id=1, source_target_pairs={{0,1},{1,2},{2,3},{4,5},{5,6},{6,7},{8,9},{9,10},{10,11},{12,13},{... | collective-permute-start | bytes 728 | tf_op jit(solution)/shard_map/ppermute | solution.py:25
  77.4 179.1 %collective-permute-start.10 = (f32[3,6,10,1]{3,2,1,0:T(8,128)S(1)}, f32[3,6,10,1]{3,2,1,0:T(8,128)S(1)}, u32[]{:S(2)}, u32[]{:S(2)}) collective-permute-start(f32[3,6,10,1]{3,2,1,0:T(8,128)S(1)} %get-tuple-element.236), channel_id=1, source_target_pairs={{1,0},{2,1},{3,2},{5,4},{6,5},{7,6},{9,8},{10,9},{11,10},{13,12},{... | collective-permute-start | bytes 2168 | tf_op jit(solution)/shard_map/ppermute | solution.py:27
  78.7 177.8 %collective-permute-start.11 = (f32[3,6,10,1]{3,2,1,0:T(8,128)S(1)}, f32[3,6,10,1]{3,2,1,0:T(8,128)S(1)}, u32[]{:S(2)}, u32[]{:S(2)}) collective-permute-start(f32[3,6,10,1]{3,2,1,0:T(8,128)S(1)} %get-tuple-element.237), channel_id=1, source_target_pairs={{0,1},{1,2},{2,3},{4,5},{5,6},{6,7},{8,9},{9,10},{10,11},{12,13},{... | collective-permute-start | bytes 2168 | tf_op jit(solution)/shard_map/ppermute | solution.py:25
  82.7 0.6 copy-start.1
  148.8 108.6 %all-to-all-start.2 = ((f32[256,3,128]{2,1,0:T(4,128)}), f32[256,3,128]{2,1,0:T(4,128)S(1)}, u32[]{:S(2)}, u32[]{:S(2)}) async-start(f32[256,3,128]{2,1,0:T(4,128)} %copy.74), calls=%async_computation.2 | async-start | bytes 1048576 | tf_op jit(solution)/shard_map/all_to_all | solution.py:122
  156.2 100.4 %copy-start = (f32[3,4,8,256]{3,2,1,0:T(8,128)S(1)}, f32[3,4,8,256]{3,2,1,0:T(8,128)}, u32[]{:S(2)}) copy-start(f32[3,4,8,256]{3,2,1,0:T(8,128)} %param.11) | copy-start | bytes 294916
where the time goes:
time: 260 us; the launch traced here: 258 us
  matrix products  139 us (53%)
  starting transfers between devices  52 us (20%)
  other arithmetic  48.3 us (19%)
  waiting for transfers between devices  10.7 us (4%)
  local copies, waits for them, and re-layouts  7 us (3%)
    dot_general x8, matrix products, add_block(): jnp.dot(plane_hot.T, spread_rows, precision=HIGH, preferred_element_type=...  77.3 us
    dot_general x4, matrix products, one_block(): jnp.dot(plane_hot, grid, precision=HIGH, preferred_element_type=jnp.float32)  59.1 us
    mul x4, other arithmetic, add_block(): value_rows.T[:, :, None] * lane_hot[:, None, :]  34 us
    ppermute x6, starting transfers between devices, extended(): lax.ppermute(tail, axis, [(i, (i + 1) % count) for i in range(ends)])  26.1 us
    ppermute x6, starting transfers between devices, extended(): lax.ppermute(head, axis, [((i + 1) % count, i) for i in range(ends)])  7.75 us
    all_to_all x1, starting transfers between devices, move_values(): lax.all_to_all(values, ('gx', 'gy'), split_axis=0, concat_axis=0, tiled=T...  7.41 us
    all_to_all x1, starting transfers between devices, move_particles(): lax.all_to_all(send_cells, ('gx', 'gy'), split_axis=0, concat_axis=0, til...  7.28 us
    all_to_all x1, waiting for transfers between devices, move_particles(): lax.all_to_all(send_cells, ('gx', 'gy'), split_axis=0, concat_axis=0, til...  6.16 us
  transfers between devices with their start and end apart: 15, of which 5 were waited for; matrix products, arithmetic and copies ran while one was open for 72% of the time, Pallas kernels for 0%

commit v1 on v0

v1 whole, which is shorter than its diff:
```python
import functools
import math

import jax
import jax.numpy as jnp
from jax import lax
from jax.experimental import pallas as pl
from jax.experimental.pallas import tpu as pltpu
from jax.sharding import PartitionSpec as P

VISCOSITY = 0.1
FLUID_DENSITY = 0.05
SOLID_DENSITY = 2.5
TIME_STEP = 0.05
VOID_FLOOR = 0.35
SPREAD = 0.1
GROUP = 8
PLANE = ("gx", "gy")
VMEM = pltpu.MemorySpace.VMEM
SMEM = pltpu.MemorySpace.SMEM


def halves(value):
    high = value.astype(jnp.bfloat16)
    low = (value - high.astype(jnp.float32)).astype(jnp.bfloat16)
    return high, low


def lane_onehot(cell_row, lane_count, per_block):
    lanes = lax.broadcasted_iota(jnp.int32, (lane_count, per_block), 0)
    hit = lanes == (cell_row & (lane_count - 1))
    return jnp.where(hit, 1.0, 0.0).astype(jnp.bfloat16)


def row_hits(cell_row, row_count, lane_count, per_block):
    rows = lax.broadcasted_iota(jnp.int32, (row_count, per_block), 0)
    return rows == lax.shift_right_logical(cell_row, lane_count.bit_length() - 1)


def spread_rows(hits, values):
    pieces = [halves(value) for value in values]
    stacked = [jnp.where(hits, part[0].astype(jnp.float32), 0.0) for part in pieces]
    stacked += [jnp.where(hits, part[1].astype(jnp.float32), 0.0) for part in pieces]
    return jnp.concatenate(stacked, axis=0).astype(jnp.bfloat16)


def onto_cells(rows, lane_hot):
    both = lax.dot_general(
        rows, lane_hot, (((1,), (1,)), ((), ())), preferred_element_type=jnp.float32
    )
    half = both.shape[0] // 2
    return both[:half] + both[half:]


def volume_kernel(owner_ref, cell_ref, diam_ref, out_ref):
    blocks, per_block = cell_ref.shape
    row_count, lane_count = out_ref.shape[1:]
    out_ref[...] = jnp.zeros_like(out_ref)

    @pl.loop(0, blocks // GROUP)
    def _(group):
        start = pl.multiple_of(group * GROUP, GROUP)
        cells = cell_ref[pl.ds(start, GROUP), :]
        diam = diam_ref[pl.ds(start, GROUP), :]
        volume = math.pi / 6 * diam * diam * diam
        adds = []
        for i in range(GROUP):
            row = cells[i : i + 1]
            hits = row_hits(row, row_count, lane_count, per_block)
            rows = spread_rows(hits, [volume[i : i + 1]])
            adds.append(onto_cells(rows, lane_onehot(row, lane_count, per_block)))
        for i in range(GROUP):
            owner = owner_ref[start + i]
            out_ref[owner] = out_ref[owner] + adds[i]


def force_kernel(
    owner_ref, cell_ref, diam_ref, part_ref, vel_ref, void_ref, accel_ref, out_ref, table
):
    blocks, per_block = cell_ref.shape
    owners, row_count, lane_count = void_ref.shape
    out_ref[...] = jnp.zeros_like(out_ref)

    @pl.loop(0, owners)
    def _(owner):
        both = jnp.concatenate([vel_ref[owner], void_ref[owner]], axis=0)
        high, low = halves(both)
        table[owner] = jnp.concatenate([high, low], axis=0)

    @pl.loop(0, blocks // GROUP)
    def _(group):
        start = pl.multiple_of(group * GROUP, GROUP)
        cells = cell_ref[pl.ds(start, GROUP), :]
        diam = diam_ref[pl.ds(start, GROUP), :]
        hots, hit_list, looked = [], [], [[], [], [], []]
        for i in range(GROUP):
            row = cells[i : i + 1]
            hot = lane_onehot(row, lane_count, per_block)
            hits = row_hits(row, row_count, lane_count, per_block)
            hots.append(hot)
            hit_list.append(hits)
            both = jnp.dot(
                table[owner_ref[start + i]], hot, preferred_element_type=jnp.float32
            )
            half = both.shape[0] // 2
            both = both[:half] + both[half:]
            for comp in range(4):
                piece = both[comp * row_count : (comp + 1) * row_count]
                looked[comp].append(
                    jnp.sum(jnp.where(hits, piece, 0.0), axis=0, keepdims=True)
                )
        at = [jnp.concatenate(rows, axis=0) for rows in looked]
        slip = [at[comp] - part_ref[pl.ds(start, GROUP), comp, :] for comp in range(3)]
        void_at = at[3]
        speed = jnp.sqrt(slip[0] * slip[0] + slip[1] * slip[1] + slip[2] * slip[2])
        reynolds = jnp.maximum(void_at * diam * speed / VISCOSITY, 1.0)
        drag_coeff = 0.63 + 4.8 / jnp.sqrt(reynolds)
        drag_coeff = drag_coeff * drag_coeff
        gap = 1.5 - jnp.log(reynolds) * (1.0 / math.log(10.0))
        chi_exp = 3.7 - 0.65 * jnp.exp(-0.5 * gap * gap)
        magnitude = 0.5 * drag_coeff * FLUID_DENSITY * (math.pi / 4) * diam * diam
        magnitude = magnitude * jnp.exp((2.0 - chi_exp) * jnp.log(void_at)) * speed
        force = [magnitude * slip[comp] for comp in range(3)]
        mass = SOLID_DENSITY * (math.pi / 6 * diam * diam * diam)
        for comp in range(3):
            accel_ref[pl.ds(start, GROUP), comp, :] = force[comp] / mass
        adds = []
        for i in range(GROUP):
            rows = spread_rows(hit_list[i], [force[comp][i : i + 1] for comp in range(3)])
            adds.append(onto_cells(rows, hots[i]))
        for i in range(GROUP):
            owner = owner_ref[start + i]
            out_ref[owner] = out_ref[owner] + adds[i]


def neighbours(padded):
    total = padded[..., 2:, 1:-1, 1:-1] + padded[..., :-2, 1:-1, 1:-1]
    total = total + padded[..., 1:-1, 2:, 1:-1] + padded[..., 1:-1, :-2, 1:-1]
    return total + padded[..., 1:-1, 1:-1, 2:] + padded[..., 1:-1, 1:-1, :-2]


def with_edges(cells):
    count = lax.axis_size("gz")
    up = [(i, i + 1) for i in range(count - 1)]
    down = [(i + 1, i) for i in range(count - 1)]
    return jnp.concatenate(
        [
            lax.ppermute(cells[..., -1:], "gz", up),
            cells,
            lax.ppermute(cells[..., :1], "gz", down),
        ],
        axis=-1,
    )


def per_device(fluid_velocity, particle_velocity, diameter, particle_cell, block_owner):
    size_x, size_y = lax.axis_size("gx"), lax.axis_size("gy")
    owners = size_x * size_y
    bx, by, lane_count = fluid_velocity.shape[1:]
    row_count = bx * by
    at_x, at_y = lax.axis_index("gx") * bx, lax.axis_index("gy") * by
    owner_list = block_owner[:, 0]
    limit = 56 * 1024 * 1024

    partial = pl.pallas_call(
        volume_kernel,
        out_shape=jax.ShapeDtypeStruct((owners, row_count, lane_count), jnp.float32),
        in_specs=[pl.BlockSpec(memory_space=SMEM)] + [pl.BlockSpec(memory_space=VMEM)] * 2,
        out_specs=pl.BlockSpec(memory_space=VMEM),
        compiler_params=pltpu.CompilerParams(vmem_limit_bytes=limit),
        name="volume_deposit",
    )(owner_list, particle_cell, diameter)

    vel_edges = with_edges(fluid_velocity)
    vel_all = lax.all_gather(fluid_velocity.reshape(3 * row_count, lane_count), PLANE)

    parts = lax.all_to_all(partial, PLANE, split_axis=0, concat_axis=0, tiled=True)
    solid = jnp.sum(parts, axis=0).reshape(bx, by, lane_count)
    solid_all = lax.all_gather(with_edges(solid), PLANE)
    plane = solid_all.reshape(size_x, size_y, bx, by, lane_count + 2)
    plane = plane.transpose(0, 2, 1, 3, 4).reshape(size_x * bx, size_y * by, lane_count + 2)
    plane = jnp.pad(plane, ((1, 1), (1, 1), (0, 0)))
    smooth = (plane[1:-1, 1:-1, 1:-1] + SPREAD * neighbours(plane)) / (1.0 + 6 * SPREAD)
    void_plane = jnp.maximum(1.0 - smooth, VOID_FLOOR)
    voidage = lax.dynamic_slice(void_plane, (at_x, at_y, 0), (bx, by, lane_count))
    void_all = void_plane.reshape(size_x, bx, size_y, by, lane_count)
    void_all = void_all.transpose(0, 2, 1, 3, 4).reshape(owners, row_count, lane_count)

    accel, force_part = pl.pallas_call(
        force_kernel,
        out_shape=(
            jax.ShapeDtypeStruct(particle_velocity.shape, jnp.float32),
            jax.ShapeDtypeStruct((owners, 3 * row_count, lane_count), jnp.float32),
        ),
        in_specs=[pl.BlockSpec(memory_space=SMEM)] + [pl.BlockSpec(memory_space=VMEM)] * 5,
        out_specs=(pl.BlockSpec(memory_space=VMEM),) * 2,
        scratch_shapes=[pltpu.VMEM((owners, 8 * row_count, lane_count), jnp.bfloat16)],
        compiler_params=pltpu.CompilerParams(vmem_limit_bytes=limit),
        name="force_deposit",
    )(owner_list, particle_cell, diameter, particle_velocity, vel_all, void_all)

    forces = lax.all_to_all(force_part, PLANE, split_axis=0, concat_axis=0, tiled=True)
    source = -jnp.sum(forces, axis=0).reshape(3, bx, by, lane_count)

    vel_plane = vel_all.reshape(size_x, size_y, 3, bx, by, lane_count)
    vel_plane = vel_plane.transpose(2, 0, 3, 1, 4, 5)
    vel_plane = vel_plane.reshape(3, size_x * bx, size_y * by, lane_count)
    vel_plane = jnp.pad(vel_plane, ((0, 0), (1, 1), (1, 1), (0, 0)))
    near = lax.dynamic_slice(
        vel_plane, (0, at_x, at_y, 0), (3, bx + 2, by + 2, lane_count)
    )
    total = near[:, 2:, 1:-1] + near[:, :-2, 1:-1] + near[:, 1:-1, 2:] + near[:, 1:-1, :-2]
    total = total + vel_edges[..., 2:] + vel_edges[..., :-2]
    laplace = total - 6.0 * fluid_velocity
    fluid_next = fluid_velocity + TIME_STEP * (laplace + source / (FLUID_DENSITY * voidage)[None])
    return (accel, voidage, fluid_next)


def solution(mesh):
    placed = (
        P(None, "gx", "gy", "gz"),
        P(("gx", "gy", "gz"), None, None),
        P(("gx", "gy", "gz"), None),
        P(("gx", "gy", "gz"), None),
        P(("gx", "gy", "gz"), None),
    )
    return jax.shard_map(
        per_device,
        mesh=mesh,
        in_specs=placed,
        out_specs=(
            P(("gx", "gy", "gz"), None, None),
            P("gx", "gy", "gz"),
            P(None, "gx", "gy", "gz"),
        ),
        check_vma=False,
    )
```

time: 260 us -> 118 us (0.45)
  matrix products: 139 us -> 0 us
  blocking collectives: 0 us -> 68.1 us
  other arithmetic: 48.3 us -> 2.06 us
  starting transfers between devices: 52 us -> 18 us
  Pallas kernels: 0 us -> 13.4 us
  local copies, waits for them, and re-layouts: 7 us -> 2.56 us
    dot_general x14 -> x0, matrix products: 139 us -> none  [the longest x8 77.3 us: add_block(): jnp.dot(plane_hot.T, spread_rows, precision=HIGH, preferred_element_type=...]
    all_gather x0 -> x2, blocking collectives: none -> 68.1 us  [the longest x1 37 us: per_device(): lax.all_gather(fluid_velocity.reshape(3 * row_count, lane_count), PLANE)]
    mul x8 -> x0, other arithmetic: 35.2 us -> none  [the longest x4 34 us: add_block(): value_rows.T[:, :, None] * lane_hot[:, None, :]]
    ppermute x12 -> x4, starting transfers between devices: 33.8 us -> 6.89 us  [the longest x2 4.32 us: with_edges(): lax.ppermute(cells[..., -1:], 'gz', up)]
    pallas_call x0 -> x2, Pallas kernels: none -> 13.4 us  [the longest x1 9.37 us: per_device(): pl.pallas_call(force_kernel, out_shape=(jax.ShapeDtypeStruct(particle_vel...]
    convert_element_type x10 -> x0, other arithmetic: 9.17 us -> none  [the longest x4 3.89 us: one_block(): lane_hot = (cell_rows[:, None] % lane_count == jnp.arange(lane_count, dty...]
    all_to_all x3 -> x2, starting transfers between devices: 18.2 us -> 11.1 us  [the longest x1 7.43 us: per_device(): lax.all_to_all(partial, PLANE, split_axis=0, concat_axis=0, tiled=True)]
    all_to_all x3 -> x2, waiting for transfers between devices: 6.17 us -> 12.2 us  [the longest x1 12.2 us: per_device(): lax.all_to_all(force_part, PLANE, split_axis=0, concat_axis=0, tiled=True)]
  transfers between devices with their start and end apart: 15 -> 6, of which waited for: 5 -> 2; matrix products, arithmetic and copies ran while one was open for 72% -> 2% of each run, Pallas kernels for 0% -> 0%
where the time goes in v1:
time: 118 us; the launch traced here: 117 us
  blocking collectives  68.1 us (58%)
  starting transfers between devices  18 us (15%)
  Pallas kernels  13.4 us (11%)
  waiting for transfers between devices  12.2 us (10%)
  local copies, waits for them, and re-layouts  2.56 us (2%)
  other arithmetic  2.06 us (2%)
    all_gather x1, blocking collectives, per_device(): lax.all_gather(fluid_velocity.reshape(3 * row_count, lane_count), PLANE)  37 us
    all_gather x1, blocking collectives, per_device(): solid_all = lax.all_gather(with_edges(solid), PLANE)  31.1 us
    all_to_all x1, waiting for transfers between devices, per_device(): lax.all_to_all(force_part, PLANE, split_axis=0, concat_axis=0, tiled=True)  12.2 us
    pallas_call x1, Pallas kernels, per_device(): pl.pallas_call(force_kernel, out_shape=(jax.ShapeDtypeStruct(particle_vel...  9.37 us
    all_to_all x1, starting transfers between devices, per_device(): lax.all_to_all(partial, PLANE, split_axis=0, concat_axis=0, tiled=True)  7.43 us
    ppermute x2, starting transfers between devices, with_edges(): lax.ppermute(cells[..., -1:], 'gz', up)  4.32 us
    pallas_call x1, Pallas kernels, per_device(): pl.pallas_call(volume_kernel, out_shape=jax.ShapeDtypeStruct((owners, row...  4.01 us
    all_to_all x1, starting transfers between devices, per_device(): lax.all_to_all(force_part, PLANE, split_axis=0, concat_axis=0, tiled=True)  3.68 us
  transfers between devices with their start and end apart: 6, of which 2 were waited for; matrix products, arithmetic and copies ran while one was open for 2% of the time, Pallas kernels for 0%

profile of v1, /device:TPU:0, one launch (start us, length us, event | category | flops | bytes accessed | tf_op | source)
XLA Modules:
  0.0 117.1 jit_solution(14140890899363976336)
XLA Ops:
  0.6 0.0 copy-start.1
  0.6 4.0 %volume_deposit.1 = f32[8,32,256]{2,1,0:T(8,128)} custom-call(s32[64]{0:T(128)} %bitcast.26, s32[64,128]{1,0:T(8,128)} %cell_ref.3, f32[64,128]{1,0:T(8,128)} %diam_ref.3), custom_call_target="tpu_custom_call" | custom-call | tf_op jit(solution)/shard_map/volume_deposit/pallas_call | solution.py:165
  4.6 0.0 copy-start.3
  4.6 7.4 %all-to-all-start = ((f32[8,32,256]{2,1,0:T(8,128)}), f32[8,32,256]{2,1,0:T(8,128)S(1)}, u32[]{:S(2)}, u32[]{:S(2)}) async-start(f32[8,32,256]{2,1,0:T(8,128)} %volume_deposit.1), calls=%async_computation | async-start | bytes 524288 | tf_op jit(solution)/shard_map/all_to_all | solution.py:177
  12.1 0.0 copy-done.1
  12.1 37.0 %all_gather.9.vel_ref = f32[8,96,256]{2,1,0:T(8,128)} all-gather(f32[1,96,256]{2,1,0:T(8,128)S(1)} %bitcast.22), channel_id=1, replica_groups=mesh['gx'=4,'gy'=2,'gz'=4] {'gx','gy'}, dimensions={0}, use_global_device_ids=true | all-gather | bytes 884736 | tf_op jit(solution)/shard_map/all_gather | solution.py:175
  49.1 0.0 all-to-all-done
  49.1 0.1 fusion.18
  49.2 1.3 %collective-permute-start.1 = (f32[4,8,1]{2,1,0:T(8,128)S(1)}, f32[4,8,1]{2,1,0:T(8,128)S(1)}, u32[]{:S(2)}, u32[]{:S(2)}) collective-permute-start(f32[4,8,1]{2,1,0:T(8,128)S(1)} %get-tuple-element.24), channel_id=1, source_target_pairs={{1,0},{2,1},{3,2},{5,4},{6,5},{7,6},{9,8},{10,9},{11,10},{13,12},{... | collective-permute-start | bytes 392 | tf_op jit(solution)/shard_map/ppermute | solution.py:150
  50.5 3.0 %collective-permute-start = (f32[4,8,1]{2,1,0:T(8,128)S(1)}, f32[4,8,1]{2,1,0:T(8,128)S(1)}, u32[]{:S(2)}, u32[]{:S(2)}) collective-permute-start(f32[4,8,1]{2,1,0:T(8,128)S(1)} %get-tuple-element.23), channel_id=1, source_target_pairs={{0,1},{1,2},{2,3},{4,5},{5,6},{6,7},{8,9},{9,10},{10,11},{12,13},{... | collective-permute-start | bytes 392 | tf_op jit(solution)/shard_map/ppermute | solution.py:148
  53.5 0.0 copy-done.3
  53.5 0.7 copy.23.part_ref
  54.3 0.0 collective-permute-done.1
  54.3 0.1 collective-permute-done
  54.3 0.1 pad_maximum_fusion.2
  54.4 31.1 %all-gather = f32[32,8,258]{2,1,0:T(8,128)S(1)} all-gather(f32[4,8,258]{2,1,0:T(8,128)S(1)} %pad_maximum_fusion.2), channel_id=2, replica_groups=mesh['gx'=4,'gy'=2,'gz'=4] {'gx','gy'}, dimensions={0}, use_global_device_ids=true | all-gather | bytes 297216 | tf_op jit(solution)/shard_map/all_gather | solution.py:179
  85.5 0.5 fusion.9
  86.0 0.7 copy.22
  86.7 9.4 %force_deposit.1 = (f32[64,3,128]{2,1,0:T(4,128)}, f32[8,96,256]{2,1,0:T(8,128)}) custom-call(s32[64]{0:T(128)} %bitcast.27, s32[64,128]{1,0:T(8,128)} %cell_ref.3, f32[64,128]{1,0:T(8,128)} %diam_ref.3, f32[64,3,128]{2,1,0:T(4,128)} %copy.23.part_ref, f32[8,96,256]{2,1,0:T(8,128)} %all_gather.9.vel_ref, f32[8,32,256]{2,1,0:T(8,128)} %bitcast.21), custom_call_target="tpu_custom_call" | custom-call | tf_op jit(solution)/shard_map/force_deposit/pallas_call | solution.py:189
  96.1 0.0 copy-start
  96.1 3.7 %all-to-all-start.1 = ((f32[8,96,256]{2,1,0:T(8,128)}), f32[8,96,256]{2,1,0:T(8,128)S(1)}, u32[]{:S(2)}, u32[]{:S(2)}) async-start(f32[8,96,256]{2,1,0:T(8,128)} %get-tuple-element.6), calls=%async_computation.1 | async-start | bytes 1572864 | tf_op jit(solution)/shard_map/all_to_all | solution.py:202
  99.8 0.1 fusion.17
  99.9 1.3 %collective-permute-start.3 = (f32[3,4,8,1]{3,2,1,0:T(8,128)S(1)}, f32[3,4,8,1]{3,2,1,0:T(8,128)S(1)}, u32[]{:S(2)}, u32[]{:S(2)}) collective-permute-start(f32[3,4,8,1]{3,2,1,0:T(8,128)S(1)} %get-tuple-element.22), channel_id=1, source_target_pairs={{0,1},{1,2},{2,3},{4,5},{5,6},{6,7},{8,9},{9,10},{10,11},{12,13},{... | collective-permute-start | bytes 1160 | tf_op jit(solution)/shard_map/ppermute | solution.py:148
  101.2 1.3 %collective-permute-start.2 = (f32[3,4,8,1]{3,2,1,0:T(8,128)S(1)}, f32[3,4,8,1]{3,2,1,0:T(8,128)S(1)}, u32[]{:S(2)}, u32[]{:S(2)}) collective-permute-start(f32[3,4,8,1]{3,2,1,0:T(8,128)S(1)} %get-tuple-element.21), channel_id=1, source_target_pairs={{1,0},{2,1},{3,2},{5,4},{6,5},{7,6},{9,8},{10,9},{11,10},{13,12},{... | collective-permute-start | bytes 1160 | tf_op jit(solution)/shard_map/ppermute | solution.py:150
  102.5 0.0 copy-done
  102.5 0.0 copy-start.2
  102.5 0.1 copy.24
  102.6 0.6 broadcast_multiply_fusion
  103.2 0.2 copy-done.2
  103.4 0.6 copy.25
  104.0 12.2 %all-to-all-done.1 = f32[8,96,256]{2,1,0:T(8,128)S(1)} async-done(((f32[8,96,256]{2,1,0:T(8,128)}), f32[8,96,256]{2,1,0:T(8,128)S(1)}, u32[]{:S(2)}, u32[]{:S(2)}) %all-to-all-start.1) | async-done | bytes 786464 | tf_op jit(solution)/shard_map/all_to_all | solution.py:202
  116.2 0.1 reduce_sum.19
  116.3 0.0 collective-permute-done.3
  116.3 0.0 collective-permute-done.2
  116.3 0.8 multiply_add_fusion
  (3 shorter events, 0.1 us)
Async XLA Ops:
  0.6 11.4 %copy-start.1 = (f32[3,4,8,256]{3,2,1,0:T(8,128)S(1)}, f32[3,4,8,256]{3,2,1,0:T(8,128)}, u32[]{:S(2)}) copy-start(f32[3,4,8,256]{3,2,1,0:T(8,128)} %param.5) | copy-start | bytes 294916
  4.6 48.9 %copy-start.3 = (f32[64,3,128]{2,0,1:T(8,128)S(1)}, f32[64,3,128]{2,0,1:T(8,128)}, u32[]{:S(2)}) copy-start(f32[64,3,128]{2,0,1:T(8,128)} %param.6) | copy-start | bytes 294916
  4.6 44.4 %all-to-all-start = ((f32[8,32,256]{2,1,0:T(8,128)}), f32[8,32,256]{2,1,0:T(8,128)S(1)}, u32[]{:S(2)}, u32[]{:S(2)}) async-start(f32[8,32,256]{2,1,0:T(8,128)} %volume_deposit.1), calls=%async_computation | async-start | bytes 524288 | tf_op jit(solution)/shard_map/all_to_all | solution.py:177
  49.2 5.1 %collective-permute-start.1 = (f32[4,8,1]{2,1,0:T(8,128)S(1)}, f32[4,8,1]{2,1,0:T(8,128)S(1)}, u32[]{:S(2)}, u32[]{:S(2)}) collective-permute-start(f32[4,8,1]{2,1,0:T(8,128)S(1)} %get-tuple-element.24), channel_id=1, source_target_pairs={{1,0},{2,1},{3,2},{5,4},{6,5},{7,6},{9,8},{10,9},{11,10},{13,12},{... | collective-permute-start | bytes 392 | tf_op jit(solution)/shard_map/ppermute | solution.py:150
  50.5 3.9 %collective-permute-start = (f32[4,8,1]{2,1,0:T(8,128)S(1)}, f32[4,8,1]{2,1,0:T(8,128)S(1)}, u32[]{:S(2)}, u32[]{:S(2)}) collective-permute-start(f32[4,8,1]{2,1,0:T(8,128)S(1)} %get-tuple-element.23), channel_id=1, source_target_pairs={{0,1},{1,2},{2,3},{4,5},{5,6},{6,7},{8,9},{9,10},{10,11},{12,13},{... | collective-permute-start | bytes 392 | tf_op jit(solution)/shard_map/ppermute | solution.py:148
  96.1 6.4 %copy-start = (f32[8,96,256]{2,1,0:T(8,128)S(1)}, f32[8,96,256]{2,1,0:T(8,128)}, u32[]{:S(2)}) copy-start(f32[8,96,256]{2,1,0:T(8,128)} %all_gather.9.vel_ref) | copy-start | bytes 2359300
  96.1 20.1 %all-to-all-start.1 = ((f32[8,96,256]{2,1,0:T(8,128)}), f32[8,96,256]{2,1,0:T(8,128)S(1)}, u32[]{:S(2)}, u32[]{:S(2)}) async-start(f32[8,96,256]{2,1,0:T(8,128)} %get-tuple-element.6), calls=%async_computation.1 | async-start | bytes 1572864 | tf_op jit(solution)/shard_map/all_to_all | solution.py:202
  99.9 16.4 %collective-permute-start.3 = (f32[3,4,8,1]{3,2,1,0:T(8,128)S(1)}, f32[3,4,8,1]{3,2,1,0:T(8,128)S(1)}, u32[]{:S(2)}, u32[]{:S(2)}) collective-permute-start(f32[3,4,8,1]{3,2,1,0:T(8,128)S(1)} %get-tuple-element.22), channel_id=1, source_target_pairs={{0,1},{1,2},{2,3},{4,5},{5,6},{6,7},{8,9},{9,10},{10,11},{12,13},{... | collective-permute-start | bytes 1160 | tf_op jit(solution)/shard_map/ppermute | solution.py:148
  101.2 15.1 %collective-permute-start.2 = (f32[3,4,8,1]{3,2,1,0:T(8,128)S(1)}, f32[3,4,8,1]{3,2,1,0:T(8,128)S(1)}, u32[]{:S(2)}, u32[]{:S(2)}) collective-permute-start(f32[3,4,8,1]{3,2,1,0:T(8,128)S(1)} %get-tuple-element.21), channel_id=1, source_target_pairs={{1,0},{2,1},{3,2},{5,4},{6,5},{7,6},{9,8},{10,9},{11,10},{13,12},{... | collective-permute-start | bytes 1160 | tf_op jit(solution)/shard_map/ppermute | solution.py:150
  102.5 0.9 copy-start.2

commit v2 on v1

--- a/solution.py
+++ b/solution.py
@@ -133,87 +133,338 @@
             out_ref[owner] = out_ref[owner] + adds[i]
 
 
-def neighbours(padded):
-    total = padded[..., 2:, 1:-1, 1:-1] + padded[..., :-2, 1:-1, 1:-1]
-    total = total + padded[..., 1:-1, 2:, 1:-1] + padded[..., 1:-1, :-2, 1:-1]
-    return total + padded[..., 1:-1, 1:-1, 2:] + padded[..., 1:-1, 1:-1, :-2]
-
-
-def with_edges(cells):
-    count = lax.axis_size("gz")
-    up = [(i, i + 1) for i in range(count - 1)]
-    down = [(i + 1, i) for i in range(count - 1)]
-    return jnp.concatenate(
-        [
-            lax.ppermute(cells[..., -1:], "gz", up),
-            cells,
-            lax.ppermute(cells[..., :1], "gz", down),
-        ],
-        axis=-1,
-    )
+def each(first, last, body):
+    def step(i, carry):
+        body(i)
+        return carry
+
+    lax.fori_loop(first, last, step, 0)
+
+
+def remote(src, dst, send_sem, recv_sem, device):
+    return pltpu.make_async_remote_copy(
+        src_ref=src,
+        dst_ref=dst,
+        send_sem=send_sem,
+        recv_sem=recv_sem,
+        device_id=device,
+        device_id_type=pl.DeviceIdType.MESH,
+    )
+
+
+def signal(semaphore, device):
+    pl.semaphore_signal(
+        semaphore, inc=1, device_id=device, device_id_type=pl.DeviceIdType.MESH
+    )
+
+
+def shifted(cells, axis, step, outside):
+    size = cells.shape[axis]
+    if step > 0:
+        kept = lax.slice_in_dim(cells, 0, size - 1, axis=axis)
+        return jnp.concatenate([outside, kept], axis=axis)
+    kept = lax.slice_in_dim(cells, 1, size, axis=axis)
+    return jnp.concatenate([kept, outside], axis=axis)
+
+
+def lane_shifted(cells, step, outside):
+    size = cells.shape[1]
+    lanes = lax.broadcasted_iota(jnp.int32, cells.shape, 1)
+    free = 0 if step > 0 else size - 1
+    return jnp.where(lanes == free, outside, pltpu.roll(cells, step % size, axis=1))
+
+
+def gather_kernel(
+    sizes,
+    partial_ref,
+    vel_ref,
+    vel_all,
+    void_all,
+    void_own,
+    base_ref,
+    parts,
+    solid_all,
+    my_edge,
+    edge_lo,
+    edge_hi,
+    vel_lo,
+    vel_hi,
+    part_send,
+    part_recv,
+    vel_send,
+    vel_recv,
+    solid_send,
+    solid_recv,
+    edge_send,
+    edge_recv,
+    side_send,
+    side_recv,
+):
+    size_x, size_y, size_z, bx, by = sizes
+    owners = size_x * size_y
+    row_count, lane_count = partial_ref.shape[1:]
+    gx, gy, gz = (lax.axis_index(name) for name in ("gx", "gy", "gz"))
+    me = gx * size_y + gy
+    above, below = lax.rem(gz + 1, size_z), lax.rem(gz + size_z - 1, size_z)
+
+    def at(owner, plane):
+        return (owner // size_y, lax.rem(owner, size_y), plane)
+
+    def slot(owner):
+        return solid_all.at[owner // size_y + 1, lax.rem(owner, size_y) + 1]
+
+    barrier = pltpu.get_barrier_semaphore()
+    each(1, owners, lambda r: signal(barrier, at(lax.rem(me + r, owners), gz)))
+    each(0, owners, lambda r: signal(barrier, at(lax.rem(me + r, owners), above)))
+    each(0, owners, lambda r: signal(barrier, at(lax.rem(me + r, owners), below)))
+    solid_all[...] = jnp.zeros_like(solid_all)
+    pl.semaphore_wait(barrier, 3 * owners - 1)
+
+    def part_copy(there, mine):
+        return remote(
+            partial_ref.at[there],
+            parts.at[mine],
+            part_send.at[there],
+            part_recv.at[mine],
+            at(there, gz),
+        )
+
+    def vel_copy(there, mine):
+        return remote(
+            vel_ref, vel_all.at[mine], vel_send.at[there], vel_recv.at[mine], at(there, gz)
+        )
+
+    def solid_copy(there, mine):
+        return remote(
+            slot(mine), slot(mine), solid_send.at[there], solid_recv.at[mine], at(there, gz)
+        )
+
+    def edge_copy(there, mine, side):
+        return remote(
+            my_edge,
+            (edge_lo, edge_hi)[side].at[mine],
+            edge_send.at[side, there],
+            edge_recv.at[side, mine],
+            at(there, (above, below)[side]),
+        )
+
+    sides = (
+        remote(
+            vel_ref.at[:, pl.ds(lane_count - 128, 128)],
+            vel_lo,
+            side_send.at[0],
+            side_recv.at[0],
+            (gx, gy, above),
+        ),
+        remote(
+            vel_ref.at[:, pl.ds(0, 128)], vel_hi, side_send.at[1], side_recv.at[1], (gx, gy, below)
+        ),
+    )
+
+    each(1, owners, lambda r: part_copy(lax.rem(me + r, owners), me).start())
+    for copy in sides:
+        copy.start()
+    each(1, owners, lambda r: vel_copy(lax.rem(me + r, owners), me).start())
+    vel_all[me] = vel_ref[...]
+
+    def add_part(r, total):
+        there = lax.rem(me + r, owners)
+        part_copy(there, there).wait_recv()
+        return total + parts[there]
+
+    solid = lax.fori_loop(1, owners, add_part, partial_ref[me])
+    rows_at = lax.broadcasted_iota(jnp.int32, (row_count, 128), 0)
+    lanes_at = lax.broadcasted_iota(jnp.int32, (row_count, 128), 1)
+    packed = [
+        jnp.sum(jnp.where(rows_at == lanes_at, column, 0.0), axis=0, keepdims=True)
+        for column in (solid[:, lane_count - 1 :], solid[:, :1])
+    ]
+    which = lax.broadcasted_iota(jnp.int32, (8, 128), 0)
+    my_edge[...] = jnp.where(which == 0, packed[0], packed[1])
+    slot(me)[...] = solid.reshape(bx, by, lane_count)
+    each(1, owners, lambda r: solid_copy(lax.rem(me + r, owners), me).start())
+    each(0, owners, lambda r: edge_copy(lax.rem(me + r, owners), me, 0).start())
+    each(0, owners, lambda r: edge_copy(lax.rem(me + r, owners), me, 1).start())
+
+    each(1, owners, lambda r: vel_copy(lax.rem(me + r, owners), lax.rem(me + r, owners)).wait_recv())
+    for copy in sides:
+        copy.wait_recv()
+    own = vel_ref[...]
+    own4 = own.reshape(3, bx, by, lane_count)
+
+    def beside(owner, there):
+        brick = vel_all[jnp.where(there, owner, me)].reshape(3, bx, by, lane_count)
+        return jnp.where(there, brick, 0.0)
+
+    x_before = beside(me - size_y, gx > 0)[:, bx - 1 :]
+    x_after = beside(me + size_y, gx < size_x - 1)[:, :1]
+    y_before = beside(me - 1, gy > 0)[:, :, by - 1 :]
+    y_after = beside(me + 1, gy < size_y - 1)[:, :, :1]
+    z_before = jnp.where(gz > 0, vel_lo[:, 127:], 0.0)
+    z_after = jnp.where(gz < size_z - 1, vel_hi[:, :1], 0.0)
+    total = shifted(own4, 1, -1, x_after) + shifted(own4, 1, 1, x_before)
+    total = total + shifted(own4, 2, -1, y_after) + shifted(own4, 2, 1, y_before)
+    total = total.reshape(3 * row_count, lane_count)
+    total = total + lane_shifted(own, -1, z_after) + lane_shifted(own, 1, z_before)
+    base_ref[...] = own + TIME_STEP * (total - 6.0 * own)
+
+    each(1, owners, lambda r: solid_copy(lax.rem(me + r, owners), lax.rem(me + r, owners)).wait_recv())
+    for side in range(2):
+        each(0, owners, lambda r, side=side: edge_copy(r, r, side).wait_recv())
+
+    def fill_brick(owner):
+        ox, oy = owner // size_y + 1, lax.rem(owner, size_y) + 1
+        cells = solid_all[ox, oy]
+        flat = cells.reshape(row_count, lane_count)
+        ends = []
+        for refs, row, inside in ((edge_lo, 0, gz > 0), (edge_hi, 1, gz < size_z - 1)):
+            line = refs[owner][row : row + 1]
+            column = jnp.sum(jnp.where(rows_at == lanes_at, line, 0.0), axis=1, keepdims=True)
+            ends.append(jnp.where(inside, column, 0.0))
+        near = shifted(cells, 0, -1, solid_all[ox + 1, oy][:1])
+        near = near + shifted(cells, 0, 1, solid_all[ox - 1, oy][bx - 1 :])
+        near = near + shifted(cells, 1, -1, solid_all[ox, oy + 1][:, :1])
+        near = near + shifted(cells, 1, 1, solid_all[ox, oy - 1][:, by - 1 :])
+        near = near.reshape(row_count, lane_count)
+        near = near + lane_shifted(flat, -1, ends[1]) + lane_shifted(flat, 1, ends[0])
+        smooth = (flat + SPREAD * near) / (1.0 + 6 * SPREAD)
+        void_all[owner] = jnp.maximum(1.0 - smooth, VOID_FLOOR)
+
+    each(0, owners, fill_brick)
+    void_own[...] = void_all[me]
+
+    def end_sends(r):
+        there = lax.rem(me + r, owners)
+        part_copy(there, me).wait_send()
+        vel_copy(there, me).wait_send()
+        solid_copy(there, me).wait_send()
+
+    each(1, owners, end_sends)
+    for side in range(2):
+        each(0, owners, lambda r, side=side: edge_copy(lax.rem(me + r, owners), me, side).wait_send())
+    for copy in sides:
+        copy.wait_send()
+
+
+def source_kernel(sizes, part_ref, base_ref, void_ref, out_ref, parts, send_sem, recv_sem):
+    size_x, size_y = sizes
+    owners = size_x * size_y
+    row_count = void_ref.shape[0]
+    gx, gy, gz = (lax.axis_index(name) for name in ("gx", "gy", "gz"))
+    me = gx * size_y + gy
+
+    def at(owner):
+        return (owner // size_y, lax.rem(owner, size_y), gz)
+
+    barrier = pltpu.get_barrier_semaphore()
+    each(1, owners, lambda r: signal(barrier, at(lax.rem(me + r, owners))))
+    pl.semaphore_wait(barrier, owners - 1)
+
+    def copy(there, mine):
+        return remote(
+            part_ref.at[there], parts.at[mine], send_sem.at[there], recv_sem.at[mine], at(there)
+        )
+
+    each(1, owners, lambda r: copy(lax.rem(me + r, owners), me).start())
+    out_ref[...] = part_ref[me]
+
+    def add(r):
+        there = lax.rem(me + r, owners)
+        copy(there, there).wait_recv()
+        out_ref[...] += parts[there]
+
+    each(1, owners, add)
+    weight = TIME_STEP / (FLUID_DENSITY * void_ref[...])
+    for comp in range(3):
+        rows = pl.ds(comp * row_count, row_count)
+        out_ref[rows, :] = base_ref[rows, :] - out_ref[rows, :] * weight
+    each(1, owners, lambda r: copy(lax.rem(me + r, owners), me).wait_send())
 
 
 def per_device(fluid_velocity, particle_velocity, diameter, particle_cell, block_owner):
-    size_x, size_y = lax.axis_size("gx"), lax.axis_size("gy")
+    size_x, size_y, size_z = (lax.axis_size(name) for name in ("gx", "gy", "gz"))
     owners = size_x * size_y
     bx, by, lane_count = fluid_velocity.shape[1:]
     row_count = bx * by
-    at_x, at_y = lax.axis_index("gx") * bx, lax.axis_index("gy") * by
     owner_list = block_owner[:, 0]
+    vmem = pl.BlockSpec(memory_space=VMEM)
+    smem = pl.BlockSpec(memory_space=SMEM)
     limit = 56 * 1024 * 1024
+
+    def full(*shape):
+        return jax.ShapeDtypeStruct(shape, jnp.float32)
 
     partial = pl.pallas_call(
         volume_kernel,
-        out_shape=jax.ShapeDtypeStruct((owners, row_count, lane_count), jnp.float32),
-        in_specs=[pl.BlockSpec(memory_space=SMEM)] + [pl.BlockSpec(memory_space=VMEM)] * 2,
-        out_specs=pl.BlockSpec(memory_space=VMEM),
+        out_shape=full(owners, row_count, lane_count),
+        in_specs=[smem] + [vmem] * 2,
+        out_specs=vmem,
         compiler_params=pltpu.CompilerParams(vmem_limit_bytes=limit),
         name="volume_deposit",
     )(owner_list, particle_cell, diameter)
 
-    vel_edges = with_edges(fluid_velocity)
-    vel_all = lax.all_gather(fluid_velocity.reshape(3 * row_count, lane_count), PLANE)
-
-    parts = lax.all_to_all(partial, PLANE, split_axis=0, concat_axis=0, tiled=True)
-    solid = jnp.sum(parts, axis=0).reshape(bx, by, lane_count)
-    solid_all = lax.all_gather(with_edges(solid), PLANE)
-    plane = solid_all.reshape(size_x, size_y, bx, by, lane_count + 2)
-    plane = plane.transpose(0, 2, 1, 3, 4).reshape(size_x * bx, size_y * by, lane_count + 2)
-    plane = jnp.pad(plane, ((1, 1), (1, 1), (0, 0)))
-    smooth = (plane[1:-1, 1:-1, 1:-1] + SPREAD * neighbours(plane)) / (1.0 + 6 * SPREAD)
-    void_plane = jnp.maximum(1.0 - smooth, VOID_FLOOR)
-    voidage = lax.dynamic_slice(void_plane, (at_x, at_y, 0), (bx, by, lane_count))
-    void_all = void_plane.reshape(size_x, bx, size_y, by, lane_count)
-    void_all = void_all.transpose(0, 2, 1, 3, 4).reshape(owners, row_count, lane_count)
+    dma = pltpu.SemaphoreType.DMA
+    vel_all, void_all, voidage, base = pl.pallas_call(
+        functools.partial(gather_kernel, (size_x, size_y, size_z, bx, by)),
+        out_shape=(
+            full(owners, 3 * row_count, lane_count),
+            full(owners, row_count, lane_count),
+            full(row_count, lane_count),
+            full(3 * row_count, lane_count),
+        ),
+        in_specs=[vmem] * 2,
+        out_specs=(vmem,) * 4,
+        scratch_shapes=[
+            pltpu.VMEM((owners, row_count, lane_count), jnp.float32),
+            pltpu.VMEM((size_x + 2, size_y + 2, bx, by, lane_count), jnp.float32),
+            pltpu.VMEM((8, 128), jnp.float32),
+            pltpu.VMEM((owners, 8, 128), jnp.float32),
+            pltpu.VMEM((owners, 8, 128), jnp.float32),
+            pltpu.VMEM((3 * row_count, 128), jnp.float32),
+            pltpu.VMEM((3 * row_count, 128), jnp.float32),
+        ]
+        + [dma((owners,))] * 6
+        + [dma((2, owners))] * 2
+        + [dma((2,))] * 2,
+        compiler_params=pltpu.CompilerParams(
+            vmem_limit_bytes=limit, collective_id=0, has_side_effects=True
+        ),
+        name="gather_plane",
+    )(partial, fluid_velocity.reshape(3 * row_count, lane_count))
 
     accel, force_part = pl.pallas_call(
         force_kernel,
         out_shape=(
             jax.ShapeDtypeStruct(particle_velocity.shape, jnp.float32),
-            jax.ShapeDtypeStruct((owners, 3 * row_count, lane_count), jnp.float32),
-        ),
-        in_specs=[pl.BlockSpec(memory_space=SMEM)] + [pl.BlockSpec(memory_space=VMEM)] * 5,
-        out_specs=(pl.BlockSpec(memory_space=VMEM),) * 2,
+            full(owners, 3 * row_count, lane_count),
+        ),
+        in_specs=[smem] + [vmem] * 5,
+        out_specs=(vmem,) * 2,
         scratch_shapes=[pltpu.VMEM((owners, 8 * row_count, lane_count), jnp.bfloat16)],
         compiler_params=pltpu.CompilerParams(vmem_limit_bytes=limit),
         name="force_deposit",
     )(owner_list, particle_cell, diameter, particle_velocity, vel_all, void_all)
 
-    forces = lax.all_to_all(force_part, PLANE, split_axis=0, concat_axis=0, tiled=True)
-    source = -jnp.sum(forces, axis=0).reshape(3, bx, by, lane_count)
-
-    vel_plane = vel_all.reshape(size_x, size_y, 3, bx, by, lane_count)
-    vel_plane = vel_plane.transpose(2, 0, 3, 1, 4, 5)
-    vel_plane = vel_plane.reshape(3, size_x * bx, size_y * by, lane_count)
-    vel_plane = jnp.pad(vel_plane, ((0, 0), (1, 1), (1, 1), (0, 0)))
-    near = lax.dynamic_slice(
-        vel_plane, (0, at_x, at_y, 0), (3, bx + 2, by + 2, lane_count)
-    )
-    total = near[:, 2:, 1:-1] + near[:, :-2, 1:-1] + near[:, 1:-1, 2:] + near[:, 1:-1, :-2]
-    total = total + vel_edges[..., 2:] + vel_edges[..., :-2]
-    laplace = total - 6.0 * fluid_velocity
-    fluid_next = fluid_velocity + TIME_STEP * (laplace + source / (FLUID_DENSITY * voidage)[None])
-    return (accel, voidage, fluid_next)
+    fluid_next = pl.pallas_call(
+        functools.partial(source_kernel, (size_x, size_y)),
+        out_shape=full(3 * row_count, lane_count),
+        in_specs=[vmem] * 3,
+        out_specs=vmem,
+        scratch_shapes=[
+            pltpu.VMEM((owners, 3 * row_count, lane_count), jnp.float32),
+            dma((owners,)),
+            dma((owners,)),
+        ],
+        compiler_params=pltpu.CompilerParams(
+            vmem_limit_bytes=limit, collective_id=1, has_side_effects=True
+        ),
+        name="sum_source",
+    )(force_part, base, voidage)
+    return (
+        accel,
+        voidage.reshape(bx, by, lane_count),
+        fluid_next.reshape(3, bx, by, lane_count),
+    )
 
 
 def solution(mesh):

time: 118 us -> 82.4 us (0.70)
  the two profiles are of different devices: /device:TPU:0 before, /device:TPU:12 now
where the time goes in v2:
time: 82.4 us; the launch traced here: 82 us
  Pallas kernels  76.1 us (92%)
  local copies, waits for them, and re-layouts  5.32 us (6%)
    pallas_call x1, Pallas kernels, per_device(): pl.pallas_call(functools.partial(gather_kernel, (size_x, size_y, size_z,...  39.5 us
    pallas_call x1, Pallas kernels, per_device(): pl.pallas_call(functools.partial(source_kernel, (size_x, size_y)), out_sh...  23.2 us
    pallas_call x1, Pallas kernels, per_device(): pl.pallas_call(force_kernel, out_shape=(jax.ShapeDtypeStruct(particle_vel...  9.36 us
    unnamed x6, local copies, waits for them, and re-layouts  5.32 us
    pallas_call x1, Pallas kernels, per_device(): pl.pallas_call(volume_kernel, out_shape=full(owners, row_count, lane_coun...  3.98 us

profile of v2, /device:TPU:12, one launch (start us, length us, event | category | flops | bytes accessed | tf_op | source)
XLA Modules:
  0.0 82.0 jit_solution(10222970756368919011)
XLA Ops:
  0.6 1.6 %copy.8.part_ref = f32[64,3,128]{2,1,0:T(4,128)} copy(f32[64,3,128]{2,0,1:T(8,128)} %param.6) | data formatting | bytes 196608 | tf_op args[1]
  2.2 4.0 %volume_deposit.1.partial_ref = f32[8,32,256]{2,1,0:T(8,128)} custom-call(s32[64]{0:T(128)} %bitcast.7, s32[64,128]{1,0:T(8,128)} %cell_ref.3, f32[64,128]{1,0:T(8,128)} %diam_ref.3), custom_call_target="tpu_custom_call" | custom-call | tf_op jit(solution)/shard_map/volume_deposit/pallas_call | solution.py:397
  6.2 39.5 %gather_plane.1 = (f32[8,96,256]{2,1,0:T(8,128)}, f32[8,32,256]{2,1,0:T(8,128)}, f32[32,256]{1,0:T(8,128)}, f32[96,256]{1,0:T(8,128)}) custom-call(f32[8,32,256]{2,1,0:T(8,128)} %volume_deposit.1.partial_ref, f32[96,256]{1,0:T(8,128)} %bitcast.6), custom_call_target="tpu_custom_call" | custom-call | tf_op jit(solution)/shard_map/gather_plane/pallas_call | solution.py:407
  45.7 9.4 %force_deposit.1 = (f32[64,3,128]{2,1,0:T(4,128)}, f32[8,96,256]{2,1,0:T(8,128)}) custom-call(s32[64]{0:T(128)} %bitcast.8, s32[64,128]{1,0:T(8,128)} %cell_ref.3, f32[64,128]{1,0:T(8,128)} %diam_ref.3, f32[64,3,128]{2,1,0:T(4,128)} %copy.8.part_ref, f32[8,96,256]{2,1,0:T(8,128)} %get-tuple-element.9.vel_ref, f32[8,32,256]{2,1,0:T(8,128)} %get-tuple-element.10.void_ref), custom_call_target="tpu_custom_call" | custom-call | tf_op jit(solution)/shard_map/force_deposit/pallas_call | solution.py:435
  55.1 1.6 %copy.9 = f32[64,3,128]{2,0,1:T(8,128)} copy(f32[64,3,128]{2,1,0:T(4,128)} %get-tuple-element.15) | data formatting | bytes 196608
  56.6 0.0 copy-start
  56.6 23.2 %sum_source.1 = f32[96,256]{1,0:T(8,128)} custom-call(f32[8,96,256]{2,1,0:T(8,128)} %get-tuple-element.13.part_ref, f32[96,256]{1,0:T(8,128)} %get-tuple-element.14.base_ref, f32[32,256]{1,0:T(8,128)} %get-tuple-element.12.void_ref), custom_call_target="tpu_custom_call" | custom-call | tf_op jit(solution)/shard_map/sum_source/pallas_call | solution.py:448
  79.9 0.0 copy-done
  79.9 0.6 copy.12
  80.5 1.5 %copy.13 = f32[3,4,8,256]{3,2,1,0:T(8,128)} copy(f32[3,4,8,256]{3,2,1,0:T(8,128)} %bitcast.4) | data formatting | bytes 196608
Async XLA Ops:
  56.6 23.2 %copy-start = (f32[32,256]{1,0:T(8,128)S(1)}, f32[32,256]{1,0:T(8,128)}, u32[]{:S(2)}) copy-start(f32[32,256]{1,0:T(8,128)} %get-tuple-element.12.void_ref) | copy-start | bytes 98308

commit v3 on v2

--- a/solution.py
+++ b/solution.py
@@ -52,26 +52,31 @@
     return both[:half] + both[half:]
 
 
-def volume_kernel(owner_ref, cell_ref, diam_ref, out_ref):
+def deposit_volume(owner_ref, cell_ref, diam_ref, out_ref):
     blocks, per_block = cell_ref.shape
-    row_count, lane_count = out_ref.shape[1:]
+    owners, row_count, lane_count = out_ref.shape
+    dense = GROUP * row_count
+    shift = lane_count.bit_length() - 1
     out_ref[...] = jnp.zeros_like(out_ref)
 
-    @pl.loop(0, blocks // GROUP)
-    def _(group):
+    def step(index):
+        group, bunch = index // (owners // GROUP), lax.rem(index, owners // GROUP)
         start = pl.multiple_of(group * GROUP, GROUP)
         cells = cell_ref[pl.ds(start, GROUP), :]
         diam = diam_ref[pl.ds(start, GROUP), :]
         volume = math.pi / 6 * diam * diam * diam
-        adds = []
+        ids = lax.broadcasted_iota(jnp.int32, (dense, per_block), 0) + bunch * dense
+        rows, hots = [], []
         for i in range(GROUP):
             row = cells[i : i + 1]
-            hits = row_hits(row, row_count, lane_count, per_block)
-            rows = spread_rows(hits, [volume[i : i + 1]])
-            adds.append(onto_cells(rows, lane_onehot(row, lane_count, per_block)))
-        for i in range(GROUP):
-            owner = owner_ref[start + i]
-            out_ref[owner] = out_ref[owner] + adds[i]
+            at = owner_ref[start + i] * row_count + lax.shift_right_logical(row, shift)
+            rows.append(spread_rows(ids == at, [volume[i : i + 1]]))
+            hots.append(lane_onehot(row, lane_count, per_block))
+        add = onto_cells(jnp.concatenate(rows, axis=1), jnp.concatenate(hots, axis=1))
+        into = pl.ds(bunch * GROUP, GROUP)
+        out_ref[into] = out_ref[into] + add.reshape(GROUP, row_count, lane_count)
+
+    each(0, (blocks // GROUP) * (owners // GROUP), step)
 
 
 def force_kernel(
@@ -110,7 +115,7 @@
                     jnp.sum(jnp.where(hits, piece, 0.0), axis=0, keepdims=True)
                 )
         at = [jnp.concatenate(rows, axis=0) for rows in looked]
-        slip = [at[comp] - part_ref[pl.ds(start, GROUP), comp, :] for comp in range(3)]
+        slip = [at[comp] - part_ref[comp, pl.ds(start, GROUP), :] for comp in range(3)]
         void_at = at[3]
         speed = jnp.sqrt(slip[0] * slip[0] + slip[1] * slip[1] + slip[2] * slip[2])
         reynolds = jnp.maximum(void_at * diam * speed / VISCOSITY, 1.0)
@@ -123,7 +128,7 @@
         force = [magnitude * slip[comp] for comp in range(3)]
         mass = SOLID_DENSITY * (math.pi / 6 * diam * diam * diam)
         for comp in range(3):
-            accel_ref[pl.ds(start, GROUP), comp, :] = force[comp] / mass
+            accel_ref[comp, pl.ds(start, GROUP), :] = force[comp] / mass
         adds = []
         for i in range(GROUP):
             rows = spread_rows(hit_list[i], [force[comp][i : i + 1] for comp in range(3)])
@@ -174,78 +179,238 @@
     return jnp.where(lanes == free, outside, pltpu.roll(cells, step % size, axis=1))
 
 
+class Plane:
+    def __init__(self, size_x, size_y):
+        self.size_x, self.size_y = size_x, size_y
+        self.gx, self.gy, self.gz = (lax.axis_index(name) for name in ("gx", "gy", "gz"))
+        self.me = self.owner(self.gx, self.gy)
+
+    def owner(self, x, y):
+        return x * self.size_y + y
+
+    def others_x(self, body):
+        each(1, self.size_x, lambda r: body(lax.rem(self.gx + r, self.size_x)))
+
+    def others_y(self, body):
+        each(1, self.size_y, lambda r: body(lax.rem(self.gy + r, self.size_y)))
+
+    def greet(self, barrier):
+        self.others_x(lambda x: signal(barrier, (x, self.gy, self.gz)))
+        self.others_y(lambda y: signal(barrier, (self.gx, y, self.gz)))
+        return self.size_x + self.size_y - 2
+
+
+class Gather:
+    def __init__(self, plane, source, slot, send_x, send_y, recv):
+        self.plane, self.source, self.slot = plane, source, slot
+        self.send_x, self.send_y, self.recv = send_x, send_y, recv
+
+    def along_x(self, x, owner):
+        p = self.plane
+        return remote(
+            self.source,
+            self.slot(owner),
+            self.send_x.at[x],
+            self.recv.at[owner],
+            (x, p.gy, p.gz),
+        )
+
+    def along_y(self, x, y, owner):
+        p = self.plane
+        return remote(
+            self.slot(owner),
+            self.slot(owner),
+            self.send_y.at[y, x],
+            self.recv.at[owner],
+            (p.gx, y, p.gz),
+        )
+
+    def start(self):
+        p = self.plane
+        p.others_x(lambda x: self.along_x(x, p.me).start())
+        p.others_y(lambda y: self.along_y(p.gx, y, p.me).start())
+
+    def forward(self):
+        p = self.plane
+
+        def pass_on(x):
+            owner = p.owner(x, p.gy)
+            self.along_x(x, owner).wait_recv()
+            p.others_y(lambda y: self.along_y(x, y, owner).start())
+
+        p.others_x(pass_on)
+
+    def wait(self):
+        p = self.plane
+
+        def arrive(y):
+            def one(r):
+                x = lax.rem(p.gx + r, p.size_x)
+                self.along_y(x, y, p.owner(x, y)).wait_recv()
+
+            each(0, p.size_x, one)
+
+        p.others_y(arrive)
+
+    def finish(self):
+        p = self.plane
+        p.others_x(lambda x: self.along_x(x, p.me).wait_send())
+
+        def one(x):
+            p.others_y(lambda y: self.along_y(x, y, p.owner(x, p.gy)).wait_send())
+
+        each(0, p.size_x, one)
+
+
+class Scatter:
+    def __init__(self, plane, source, first, middle, last, send_y, recv_y, send_x, recv_x):
+        self.plane, self.source = plane, source
+        self.first, self.middle, self.last = first, middle, last
+        self.send_y, self.recv_y, self.send_x, self.recv_x = send_y, recv_y, send_x, recv_x
+
+    def along_y(self, x, y, mine):
+        p = self.plane
+        return remote(
+            self.source.at[p.owner(x, y)],
+            self.first.at[mine, x],
+            self.send_y.at[y, x],
+            self.recv_y.at[mine, x],
+            (p.gx, y, p.gz),
+        )
+
+    def along_x(self, x, mine):
+        p = self.plane
+        return remote(
+            self.middle.at[x],
+            self.last.at[mine],
+            self.send_x.at[x],
+            self.recv_x.at[mine],
+            (x, p.gy, p.gz),
+        )
+
+    def start(self):
+        p = self.plane
+
+        def one(x):
+            p.others_y(lambda y: self.along_y(x, y, p.gy).start())
+
+        p.others_x(one)
+        one(p.gx)
+
+    def forward(self):
+        p = self.plane
+
+        def one(x):
+            self.middle[x] = self.source[p.owner(x, p.gy)]
+
+            def add(y):
+                self.along_y(x, y, y).wait_recv()
+                self.middle[x] = self.middle[x] + self.first[y, x]
+
+            p.others_y(add)
+
+        def send(x):
+            one(x)
+            self.along_x(x, p.gx).start()
+
+        p.others_x(send)
+        one(p.gx)
+
+    def total(self, out_ref):
+        p = self.plane
+        out_ref[...] = self.middle[p.gx]
+
+        def add(x):
+            self.along_x(x, x).wait_recv()
+            out_ref[...] = out_ref[...] + self.last[x]
+
+        p.others_x(add)
+
+    def finish(self):
+        p = self.plane
+
+        def one(x):
+            p.others_y(lambda y: self.along_y(x, y, p.gy).wait_send())
+
+        each(0, p.size_x, one)
+        p.others_x(lambda x: self.along_x(x, p.gx).wait_send())
+
+
+def gather_sems(size_x, size_y):
+    dma = pltpu.SemaphoreType.DMA
+    return [dma((size_x,)), dma((size_y, size_x)), dma((size_x * size_y,))]
+
+
+def scatter_scratch(size_x, size_y, rows, lanes):
+    dma = pltpu.SemaphoreType.DMA
+    return [
+        pltpu.VMEM((size_y, size_x, rows, lanes), jnp.float32),
+        pltpu.VMEM((size_x, rows, lanes), jnp.float32),
+        pltpu.VMEM((size_x, rows, lanes), jnp.float32),
+        dma((size_y, size_x)),
+        dma((size_y, size_x)),
+        dma((size_x,)),
+        dma((size_x,)),
+    ]
+
+
 def gather_kernel(
     sizes,
-    partial_ref,
+    owner_ref,
+    cell_ref,
+    diam_ref,
     vel_ref,
     vel_all,
     void_all,
     void_own,
     base_ref,
-    parts,
+    partial_ref,
+    solid_ref,
     solid_all,
     my_edge,
-    edge_lo,
-    edge_hi,
+    edges,
     vel_lo,
     vel_hi,
-    part_send,
-    part_recv,
-    vel_send,
-    vel_recv,
-    solid_send,
-    solid_recv,
     edge_send,
     edge_recv,
     side_send,
     side_recv,
+    *rest,
 ):
     size_x, size_y, size_z, bx, by = sizes
     owners = size_x * size_y
     row_count, lane_count = partial_ref.shape[1:]
-    gx, gy, gz = (lax.axis_index(name) for name in ("gx", "gy", "gz"))
-    me = gx * size_y + gy
+    plane = Plane(size_x, size_y)
+    gx, gy, gz, me = plane.gx, plane.gy, plane.gz, plane.me
     above, below = lax.rem(gz + 1, size_z), lax.rem(gz + size_z - 1, size_z)
-
-    def at(owner, plane):
-        return (owner // size_y, lax.rem(owner, size_y), plane)
 
     def slot(owner):
         return solid_all.at[owner // size_y + 1, lax.rem(owner, size_y) + 1]
 
+    def place(r, other):
+        owner = lax.rem(me + r, owners)
+        return (owner // size_y, lax.rem(owner, size_y), other)
+
     barrier = pltpu.get_barrier_semaphore()
-    each(1, owners, lambda r: signal(barrier, at(lax.rem(me + r, owners), gz)))
-    each(0, owners, lambda r: signal(barrier, at(lax.rem(me + r, owners), above)))
-    each(0, owners, lambda r: signal(barrier, at(lax.rem(me + r, owners), below)))
+    greeted = plane.greet(barrier)
+    each(0, owners, lambda r: signal(barrier, place(r, above)))
+    each(0, owners, lambda r: signal(barrier, place(r, below)))
     solid_all[...] = jnp.zeros_like(solid_all)
-    pl.semaphore_wait(barrier, 3 * owners - 1)
-
-    def part_copy(there, mine):
+    vel_all[me] = vel_ref[...]
+    pl.semaphore_wait(barrier, greeted + 2 * owners)
+
+    vel = Gather(plane, vel_ref, lambda owner: vel_all.at[owner], *rest[:3])
+    solid_gather = Gather(plane, slot(me), slot, *rest[3:6])
+    scatter = Scatter(plane, partial_ref, *rest[6:])
+
+    def edge_copy(r, mine, side):
+        there = lax.rem(me + r, owners)
         return remote(
-            partial_ref.at[there],
-            parts.at[mine],
-            part_send.at[there],
-            part_recv.at[mine],
-            at(there, gz),
-        )
-
-    def vel_copy(there, mine):
-        return remote(
-            vel_ref, vel_all.at[mine], vel_send.at[there], vel_recv.at[mine], at(there, gz)
-        )
-
-    def solid_copy(there, mine):
-        return remote(
-            slot(mine), slot(mine), solid_send.at[there], solid_recv.at[mine], at(there, gz)
-        )
-
-    def edge_copy(there, mine, side):
-        return remote(
-            my_edge,
-            (edge_lo, edge_hi)[side].at[mine],
+            my_edge.at[side],
+            edges.at[side, mine],
             edge_send.at[side, there],
             edge_recv.at[side, mine],
-            at(there, (above, below)[side]),
+            place(r, (above, below)[side]),
         )
 
     sides = (
@@ -260,33 +425,27 @@
             vel_ref.at[:, pl.ds(0, 128)], vel_hi, side_send.at[1], side_recv.at[1], (gx, gy, below)
         ),
     )
-
-    each(1, owners, lambda r: part_copy(lax.rem(me + r, owners), me).start())
+    vel.start()
     for copy in sides:
         copy.start()
-    each(1, owners, lambda r: vel_copy(lax.rem(me + r, owners), me).start())
-    vel_all[me] = vel_ref[...]
-
-    def add_part(r, total):
-        there = lax.rem(me + r, owners)
-        part_copy(there, there).wait_recv()
-        return total + parts[there]
-
-    solid = lax.fori_loop(1, owners, add_part, partial_ref[me])
+    deposit_volume(owner_ref, cell_ref, diam_ref, partial_ref)
+    scatter.start()
+    scatter.forward()
+    vel.forward()
+    scatter.total(solid_ref)
+    solid = solid_ref[...]
+    slot(me)[...] = solid.reshape(bx, by, lane_count)
+    solid_gather.start()
     rows_at = lax.broadcasted_iota(jnp.int32, (row_count, 128), 0)
     lanes_at = lax.broadcasted_iota(jnp.int32, (row_count, 128), 1)
-    packed = [
-        jnp.sum(jnp.where(rows_at == lanes_at, column, 0.0), axis=0, keepdims=True)
-        for column in (solid[:, lane_count - 1 :], solid[:, :1])
-    ]
-    which = lax.broadcasted_iota(jnp.int32, (8, 128), 0)
-    my_edge[...] = jnp.where(which == 0, packed[0], packed[1])
-    slot(me)[...] = solid.reshape(bx, by, lane_count)
-    each(1, owners, lambda r: solid_copy(lax.rem(me + r, owners), me).start())
-    each(0, owners, lambda r: edge_copy(lax.rem(me + r, owners), me, 0).start())
-    each(0, owners, lambda r: edge_copy(lax.rem(me + r, owners), me, 1).start())
-
-    each(1, owners, lambda r: vel_copy(lax.rem(me + r, owners), lax.rem(me + r, owners)).wait_recv())
+    for side, column in enumerate((solid[:, lane_count - 1 :], solid[:, :1])):
+        my_edge[side] = jnp.sum(
+            jnp.where(rows_at == lanes_at, column, 0.0), axis=0, keepdims=True
+        )
+        each(0, owners, lambda r, side=side: edge_copy(r, me, side).start())
+    solid_gather.forward()
+
+    vel.wait()
     for copy in sides:
         copy.wait_recv()
     own = vel_ref[...]
@@ -308,17 +467,17 @@
     total = total + lane_shifted(own, -1, z_after) + lane_shifted(own, 1, z_before)
     base_ref[...] = own + TIME_STEP * (total - 6.0 * own)
 
-    each(1, owners, lambda r: solid_copy(lax.rem(me + r, owners), lax.rem(me + r, owners)).wait_recv())
+    solid_gather.wait()
     for side in range(2):
-        each(0, owners, lambda r, side=side: edge_copy(r, r, side).wait_recv())
+        each(0, owners, lambda r, side=side: edge_copy(0, r, side).wait_recv())
 
     def fill_brick(owner):
         ox, oy = owner // size_y + 1, lax.rem(owner, size_y) + 1
         cells = solid_all[ox, oy]
         flat = cells.reshape(row_count, lane_count)
         ends = []
-        for refs, row, inside in ((edge_lo, 0, gz > 0), (edge_hi, 1, gz < size_z - 1)):
-            line = refs[owner][row : row + 1]
+        for side, inside in ((0, gz > 0), (1, gz < size_z - 1)):
+            line = edges[side, owner]
             column = jnp.sum(jnp.where(rows_at == lanes_at, line, 0.0), axis=1, keepdims=True)
             ends.append(jnp.where(inside, column, 0.0))
         near = shifted(cells, 0, -1, solid_all[ox + 1, oy][:1])
@@ -333,52 +492,29 @@
     each(0, owners, fill_brick)
     void_own[...] = void_all[me]
 
-    def end_sends(r):
-        there = lax.rem(me + r, owners)
-        part_copy(there, me).wait_send()
-        vel_copy(there, me).wait_send()
-        solid_copy(there, me).wait_send()
-
-    each(1, owners, end_sends)
-    for side in range(2):
-        each(0, owners, lambda r, side=side: edge_copy(lax.rem(me + r, owners), me, side).wait_send())
     for copy in sides:
         copy.wait_send()
-
-
-def source_kernel(sizes, part_ref, base_ref, void_ref, out_ref, parts, send_sem, recv_sem):
-    size_x, size_y = sizes
-    owners = size_x * size_y
+    for side in range(2):
+        each(0, owners, lambda r, side=side: edge_copy(r, me, side).wait_send())
+    vel.finish()
+    scatter.finish()
+    solid_gather.finish()
+
+
+def source_kernel(sizes, part_ref, base_ref, void_ref, out_ref, *rest):
     row_count = void_ref.shape[0]
-    gx, gy, gz = (lax.axis_index(name) for name in ("gx", "gy", "gz"))
-    me = gx * size_y + gy
-
-    def at(owner):
-        return (owner // size_y, lax.rem(owner, size_y), gz)
-
+    plane = Plane(*sizes)
     barrier = pltpu.get_barrier_semaphore()
-    each(1, owners, lambda r: signal(barrier, at(lax.rem(me + r, owners))))
-    pl.semaphore_wait(barrier, owners - 1)
-
-    def copy(there, mine):
-        return remote(
-            part_ref.at[there], parts.at[mine], send_sem.at[there], recv_sem.at[mine], at(there)
-        )
-
-    each(1, owners, lambda r: copy(lax.rem(me + r, owners), me).start())
-    out_ref[...] = part_ref[me]
-
-    def add(r):
-        there = lax.rem(me + r, owners)
-        copy(there, there).wait_recv()
-        out_ref[...] += parts[there]
-
-    each(1, owners, add)
+    pl.semaphore_wait(barrier, plane.greet(barrier))
+    scatter = Scatter(plane, part_ref, *rest)
+    scatter.start()
+    scatter.forward()
+    scatter.total(out_ref)
     weight = TIME_STEP / (FLUID_DENSITY * void_ref[...])
     for comp in range(3):
         rows = pl.ds(comp * row_count, row_count)
         out_ref[rows, :] = base_ref[rows, :] - out_ref[rows, :] * weight
-    each(1, owners, lambda r: copy(lax.rem(me + r, owners), me).wait_send())
+    scatter.finish()
 
 
 def per_device(fluid_velocity, particle_velocity, diameter, particle_cell, block_owner):
@@ -394,15 +530,6 @@
     def full(*shape):
         return jax.ShapeDtypeStruct(shape, jnp.float32)
 
-    partial = pl.pallas_call(
-        volume_kernel,
-        out_shape=full(owners, row_count, lane_count),
-        in_specs=[smem] + [vmem] * 2,
-        out_specs=vmem,
-        compiler_params=pltpu.CompilerParams(vmem_limit_bytes=limit),
-        name="volume_deposit",
-    )(owner_list, particle_cell, diameter)
-
     dma = pltpu.SemaphoreType.DMA
     vel_all, void_all, voidage, base = pl.pallas_call(
         functools.partial(gather_kernel, (size_x, size_y, size_z, bx, by)),
@@ -412,30 +539,38 @@
             full(row_count, lane_count),
             full(3 * row_count, lane_count),
         ),
-        in_specs=[vmem] * 2,
+        in_specs=[smem] + [vmem] * 3,
         out_specs=(vmem,) * 4,
         scratch_shapes=[
             pltpu.VMEM((owners, row_count, lane_count), jnp.float32),
+            pltpu.VMEM((row_count, lane_count), jnp.float32),
             pltpu.VMEM((size_x + 2, size_y + 2, bx, by, lane_count), jnp.float32),
-            pltpu.VMEM((8, 128), jnp.float32),
-            pltpu.VMEM((owners, 8, 128), jnp.float32),
-            pltpu.VMEM((owners, 8, 128), jnp.float32),
+            pltpu.VMEM((2, 1, 128), jnp.float32),
+            pltpu.VMEM((2, owners, 1, 128), jnp.float32),
             pltpu.VMEM((3 * row_count, 128), jnp.float32),
             pltpu.VMEM((3 * row_count, 128), jnp.float32),
+            dma((2, owners)),
+            dma((2, owners)),
+            dma((2,)),
+            dma((2,)),
         ]
-        + [dma((owners,))] * 6
-        + [dma((2, owners))] * 2
-        + [dma((2,))] * 2,
+        + gather_sems(size_x, size_y) * 2
+        + scatter_scratch(size_x, size_y, row_count, lane_count),
         compiler_params=pltpu.CompilerParams(
             vmem_limit_bytes=limit, collective_id=0, has_side_effects=True
         ),
         name="gather_plane",
-    )(partial, fluid_velocity.reshape(3 * row_count, lane_count))
+    )(
+        owner_list,
+        particle_cell,
+        diameter,
+        fluid_velocity.reshape(3 * row_count, lane_count),
+    )
 
     accel, force_part = pl.pallas_call(
         force_kernel,
         out_shape=(
-            jax.ShapeDtypeStruct(particle_velocity.shape, jnp.float32),
+            full(3, *diameter.shape),
             full(owners, 3 * row_count, lane_count),
         ),
         in_specs=[smem] + [vmem] * 5,
@@ -443,25 +578,21 @@
         scratch_shapes=[pltpu.VMEM((owners, 8 * row_count, lane_count), jnp.bfloat16)],
         compiler_params=pltpu.CompilerParams(vmem_limit_bytes=limit),
         name="force_deposit",
-    )(owner_list, particle_cell, diameter, particle_velocity, vel_all, void_all)
+    )(owner_list, particle_cell, diameter, particle_velocity.transpose(1, 0, 2), vel_all, void_all)
 
     fluid_next = pl.pallas_call(
         functools.partial(source_kernel, (size_x, size_y)),
         out_shape=full(3 * row_count, lane_count),
         in_specs=[vmem] * 3,
         out_specs=vmem,
-        scratch_shapes=[
-            pltpu.VMEM((owners, 3 * row_count, lane_count), jnp.float32),
-            dma((owners,)),
-            dma((owners,)),
-        ],
+        scratch_shapes=scatter_scratch(size_x, size_y, 3 * row_count, lane_count),
         compiler_params=pltpu.CompilerParams(
             vmem_limit_bytes=limit, collective_id=1, has_side_effects=True
         ),
         name="sum_source",
     )(force_part, base, voidage)
     return (
-        accel,
+        accel.transpose(1, 0, 2),
         voidage.reshape(bx, by, lane_count),
         fluid_next.reshape(3, bx, by, lane_count),
     )

time: 82.4 us -> 61.5 us (0.75)
  the two profiles are of different devices: /device:TPU:12 before, /device:TPU:0 now
where the time goes in v3:
time: 61.5 us; the launch traced here: 61.3 us
  Pallas kernels  58.5 us (95%)
  local copies, waits for them, and re-layouts  2.16 us (4%)
  between operations  0.65 us (1%)
    pallas_call x1, Pallas kernels, per_device(): pl.pallas_call(functools.partial(gather_kernel, (size_x, size_y, size_z,...  31.3 us
    pallas_call x1, Pallas kernels, per_device(): pl.pallas_call(functools.partial(source_kernel, (size_x, size_y)), out_sh...  17.9 us
    pallas_call x1, Pallas kernels, per_device(): pl.pallas_call(force_kernel, out_shape=(full(3, *diameter.shape), full(ow...  9.3 us
    unnamed x4, local copies, waits for them, and re-layouts  2.16 us

profile of v3, /device:TPU:0, one launch (start us, length us, event | category | flops | bytes accessed | tf_op | source)
XLA Modules:
  0.0 61.3 jit_solution(14229125605347127855)
XLA Ops:
  0.6 31.3 %gather_plane.1 = (f32[8,96,256]{2,1,0:T(8,128)}, f32[8,32,256]{2,1,0:T(8,128)}, f32[32,256]{1,0:T(8,128)}, f32[96,256]{1,0:T(8,128)}) custom-call(s32[64]{0:T(128)} %bitcast.10, s32[64,128]{1,0:T(8,128)} %cell_ref.3, f32[64,128]{1,0:T(8,128)} %diam_ref.3, f32[96,256]{1,0:T(8,128)} %bitcast.9), custom_call_target="tpu_custom_call" | custom-call | tf_op jit(solution)/shard_map/gather_plane/pallas_call | solution.py:534
  31.9 9.3 %force_deposit.1 = (f32[3,64,128]{2,1,0:T(8,128)}, f32[8,96,256]{2,1,0:T(8,128)}) custom-call(s32[64]{0:T(128)} %bitcast.11, s32[64,128]{1,0:T(8,128)} %cell_ref.3, f32[64,128]{1,0:T(8,128)} %diam_ref.3, f32[3,64,128]{2,1,0:T(8,128)} %bitcast.8, f32[8,96,256]{2,1,0:T(8,128)} %get-tuple-element.9.vel_ref, f32[8,32,256]{2,1,0:T(8,128)} %get-tuple-element.10.void_ref), custom_call_target="tpu_custom_call" | custom-call | tf_op jit(solution)/shard_map/force_deposit/pallas_call | solution.py:570
  41.2 0.0 copy-start
  41.2 17.9 %sum_source.1 = f32[96,256]{1,0:T(8,128)} custom-call(f32[8,96,256]{2,1,0:T(8,128)} %get-tuple-element.13.part_ref, f32[96,256]{1,0:T(8,128)} %get-tuple-element.14.base_ref, f32[32,256]{1,0:T(8,128)} %get-tuple-element.12.void_ref), custom_call_target="tpu_custom_call" | custom-call | tf_op jit(solution)/shard_map/sum_source/pallas_call | solution.py:583
  59.1 0.0 copy-done
  59.1 0.6 %copy.10 = f32[4,8,256]{2,1,0:T(8,128)} copy(f32[4,8,256]{2,1,0:T(8,128)S(1)} %bitcast.7) | data formatting | bytes 65536
  59.7 1.5 %copy.11 = f32[3,4,8,256]{3,2,1,0:T(8,128)} copy(f32[3,4,8,256]{3,2,1,0:T(8,128)} %bitcast.6) | data formatting | bytes 196608
Async XLA Ops:
  41.2 17.9 %copy-start = (f32[32,256]{1,0:T(8,128)S(1)}, f32[32,256]{1,0:T(8,128)}, u32[]{:S(2)}) copy-start(f32[32,256]{1,0:T(8,128)} %get-tuple-element.12.void_ref) | copy-start | bytes 98308

commit v4 on v3

--- a/solution.py
+++ b/solution.py
@@ -80,11 +80,22 @@
 
 
 def force_kernel(
-    owner_ref, cell_ref, diam_ref, part_ref, vel_ref, void_ref, accel_ref, out_ref, table
+    owner_ref,
+    cell_ref,
+    diam_ref,
+    part_ref,
+    vel_ref,
+    void_ref,
+    own_ref,
+    accel_ref,
+    out_ref,
+    void_out,
+    table,
 ):
     blocks, per_block = cell_ref.shape
     owners, row_count, lane_count = void_ref.shape
     out_ref[...] = jnp.zeros_like(out_ref)
+    void_out[...] = own_ref[...]
 
     @pl.loop(0, owners)
     def _(owner):
@@ -230,15 +241,16 @@
         p.others_x(lambda x: self.along_x(x, p.me).start())
         p.others_y(lambda y: self.along_y(p.gx, y, p.me).start())
 
-    def forward(self):
-        p = self.plane
-
-        def pass_on(x):
+    def forward(self, first, last):
+        p = self.plane
+
+        def pass_on(r):
+            x = lax.rem(p.gx + p.size_x - r, p.size_x)
             owner = p.owner(x, p.gy)
             self.along_x(x, owner).wait_recv()
             p.others_y(lambda y: self.along_y(x, y, owner).start())
 
-        p.others_x(pass_on)
+        each(first, last, pass_on)
 
     def wait(self):
         p = self.plane
@@ -430,8 +442,9 @@
         copy.start()
     deposit_volume(owner_ref, cell_ref, diam_ref, partial_ref)
     scatter.start()
+    vel.forward(1, size_x - 1)
     scatter.forward()
-    vel.forward()
+    vel.forward(size_x - 1, size_x)
     scatter.total(solid_ref)
     solid = solid_ref[...]
     slot(me)[...] = solid.reshape(bx, by, lane_count)
@@ -443,7 +456,7 @@
             jnp.where(rows_at == lanes_at, column, 0.0), axis=0, keepdims=True
         )
         each(0, owners, lambda r, side=side: edge_copy(r, me, side).start())
-    solid_gather.forward()
+    solid_gather.forward(1, size_x)
 
     vel.wait()
     for copy in sides:
@@ -501,8 +514,7 @@
     solid_gather.finish()
 
 
-def source_kernel(sizes, part_ref, base_ref, void_ref, out_ref, *rest):
-    row_count = void_ref.shape[0]
+def source_kernel(sizes, part_ref, out_ref, *rest):
     plane = Plane(*sizes)
     barrier = pltpu.get_barrier_semaphore()
     pl.semaphore_wait(barrier, plane.greet(barrier))
@@ -510,10 +522,6 @@
     scatter.start()
     scatter.forward()
     scatter.total(out_ref)
-    weight = TIME_STEP / (FLUID_DENSITY * void_ref[...])
-    for comp in range(3):
-        rows = pl.ds(comp * row_count, row_count)
-        out_ref[rows, :] = base_ref[rows, :] - out_ref[rows, :] * weight
     scatter.finish()
 
 
@@ -531,7 +539,7 @@
         return jax.ShapeDtypeStruct(shape, jnp.float32)
 
     dma = pltpu.SemaphoreType.DMA
-    vel_all, void_all, voidage, base = pl.pallas_call(
+    vel_all, void_all, void_own, base = pl.pallas_call(
         functools.partial(gather_kernel, (size_x, size_y, size_z, bx, by)),
         out_shape=(
             full(owners, 3 * row_count, lane_count),
@@ -567,34 +575,39 @@
         fluid_velocity.reshape(3 * row_count, lane_count),
     )
 
-    accel, force_part = pl.pallas_call(
+    accel, force_part, voidage = pl.pallas_call(
         force_kernel,
         out_shape=(
             full(3, *diameter.shape),
             full(owners, 3 * row_count, lane_count),
+            full(row_count, lane_count),
         ),
-        in_specs=[smem] + [vmem] * 5,
-        out_specs=(vmem,) * 2,
+        in_specs=[smem] + [vmem] * 6,
+        out_specs=(vmem,) * 3,
         scratch_shapes=[pltpu.VMEM((owners, 8 * row_count, lane_count), jnp.bfloat16)],
         compiler_params=pltpu.CompilerParams(vmem_limit_bytes=limit),
         name="force_deposit",
-    )(owner_list, particle_cell, diameter, particle_velocity.transpose(1, 0, 2), vel_all, void_all)
-
-    fluid_next = pl.pallas_call(
+    )(owner_list, particle_cell, diameter, particle_velocity.transpose(1, 0, 2), vel_all, void_all, void_own)
+
+    total = pl.pallas_call(
         functools.partial(source_kernel, (size_x, size_y)),
         out_shape=full(3 * row_count, lane_count),
-        in_specs=[vmem] * 3,
+        in_specs=[vmem],
         out_specs=vmem,
         scratch_shapes=scatter_scratch(size_x, size_y, 3 * row_count, lane_count),
         compiler_params=pltpu.CompilerParams(
             vmem_limit_bytes=limit, collective_id=1, has_side_effects=True
         ),
         name="sum_source",
-    )(force_part, base, voidage)
+    )(force_part)
+    voidage = voidage.reshape(bx, by, lane_count)
+    brick = (3, bx, by, lane_count)
+    weight = TIME_STEP / (FLUID_DENSITY * voidage)
+    fluid_next = base.reshape(brick) - total.reshape(brick) * weight[None]
     return (
         accel.transpose(1, 0, 2),
-        voidage.reshape(bx, by, lane_count),
-        fluid_next.reshape(3, bx, by, lane_count),
+        voidage,
+        fluid_next,
     )
 
 

time: 61.5 us -> 61.4 us (level)
  other arithmetic: 0 us -> 2.32 us
  local copies, waits for them, and re-layouts: 2.16 us -> 0.01 us
    unnamed x4 -> x2, local copies, waits for them, and re-layouts: 2.16 us -> 0.01 us
    pallas_call x1, Pallas kernels: 17.9 us -> 16.3 us  [per_device(): pl.pallas_call(functools.partial(source_kernel, (size_x, size_y)), out_sh...]
    sub x0 -> x1, other arithmetic: none -> 1.55 us  [per_device(): fluid_next = base.reshape(brick) - total.reshape(brick) * weight[None]]
    pallas_call x1, Pallas kernels: 31.3 us -> 32.5 us  [per_device(): pl.pallas_call(functools.partial(gather_kernel, (size_x, size_y, size_z,...]
    div x0 -> x1, other arithmetic: none -> 0.77 us  [per_device(): weight = TIME_STEP / (FLUID_DENSITY * voidage)]
where the time goes in v4:
time: 61.4 us; the launch traced here: 61.1 us
  Pallas kernels  58.1 us (95%)
  other arithmetic  2.32 us (4%)
  between operations  0.67 us (1%)
    pallas_call x1, Pallas kernels, per_device(): pl.pallas_call(functools.partial(gather_kernel, (size_x, size_y, size_z,...  32.5 us
    pallas_call x1, Pallas kernels, per_device(): pl.pallas_call(functools.partial(source_kernel, (size_x, size_y)), out_sh...  16.3 us
    pallas_call x1, Pallas kernels, per_device(): pl.pallas_call(force_kernel, out_shape=(full(3, *diameter.shape), full(ow...  9.31 us
    sub x1, other arithmetic, per_device(): fluid_next = base.reshape(brick) - total.reshape(brick) * weight[None]  1.55 us

profile of v4, /device:TPU:0, one launch (start us, length us, event | category | flops | bytes accessed | tf_op | source)
XLA Modules:
  0.0 61.1 jit_solution(9325031118206313665)
XLA Ops:
  0.6 32.5 %gather_plane.1 = (f32[8,96,256]{2,1,0:T(8,128)}, f32[8,32,256]{2,1,0:T(8,128)}, f32[32,256]{1,0:T(8,128)}, f32[96,256]{1,0:T(8,128)}) custom-call(s32[64]{0:T(128)} %bitcast.13, s32[64,128]{1,0:T(8,128)} %cell_ref.3, f32[64,128]{1,0:T(8,128)} %diam_ref.3, f32[96,256]{1,0:T(8,128)} %bitcast.10), custom_call_target="tpu_custom_call" | custom-call | tf_op jit(solution)/shard_map/gather_plane/pallas_call | solution.py:542
  33.2 9.3 %force_deposit.1 = (f32[3,64,128]{2,1,0:T(8,128)}, f32[8,96,256]{2,1,0:T(8,128)}, f32[32,256]{1,0:T(8,128)}) custom-call(s32[64]{0:T(128)} %bitcast.14, s32[64,128]{1,0:T(8,128)} %cell_ref.3, f32[64,128]{1,0:T(8,128)} %diam_ref.3, f32[3,64,128]{2,1,0:T(8,128)} %bitcast.9, f32[8,96,256]{2,1,0:T(8,128)} %get-tuple-element.10.vel_ref, ...), custom_call_target="tpu_custom_call" | custom-call | tf_op jit(solution)/shard_map/force_deposit/pallas_call | solution.py:578
  42.5 0.8 %multiply_divide_fusion = f32[4,8,256]{2,1,0:T(8,128)S(1)} fusion(f32[32,256]{1,0:T(8,128)} %get-tuple-element.14), kind=kLoop, calls=%fused_computation.1 | loop fusion | flops 16384 | bytes 65536 | tf_op jit(solution)/shard_map/div | solution.py:605
  43.2 0.0 copy-start
  43.2 16.3 %sum_source.1 = f32[96,256]{1,0:T(8,128)} custom-call(f32[8,96,256]{2,1,0:T(8,128)} %get-tuple-element.16.part_ref), custom_call_target="tpu_custom_call" | custom-call | tf_op jit(solution)/shard_map/sum_source/pallas_call | solution.py:592
  59.5 0.0 copy-done
  59.5 1.5 %multiply_subtract_fusion = f32[3,4,8,256]{3,2,1,0:T(8,128)} fusion(f32[3,4,8,256]{3,2,1,0:T(8,128)S(1)} %bitcast.11, f32[3,4,8,256]{3,2,1,0:T(8,128)} %bitcast.8, f32[4,8,256]{2,1,0:T(8,128)S(1)} %multiply_divide_fusion), kind=kLoop, calls=%fused_computation | loop fusion | flops 49152 | bytes 327680 | tf_op jit(solution)/shard_map/sub | solution.py:606
Async XLA Ops:
  43.2 16.3 %copy-start = (f32[96,256]{1,0:T(8,128)S(1)}, f32[96,256]{1,0:T(8,128)}, u32[]{:S(2)}) copy-start(f32[96,256]{1,0:T(8,128)} %get-tuple-element.15) | copy-start | bytes 294916

commit v5 on v4

--- a/solution.py
+++ b/solution.py
@@ -88,13 +88,12 @@
     void_ref,
     own_ref,
     accel_ref,
-    out_ref,
+    force_ref,
     void_out,
     table,
 ):
     blocks, per_block = cell_ref.shape
     owners, row_count, lane_count = void_ref.shape
-    out_ref[...] = jnp.zeros_like(out_ref)
     void_out[...] = own_ref[...]
 
     @pl.loop(0, owners)
@@ -108,13 +107,11 @@
         start = pl.multiple_of(group * GROUP, GROUP)
         cells = cell_ref[pl.ds(start, GROUP), :]
         diam = diam_ref[pl.ds(start, GROUP), :]
-        hots, hit_list, looked = [], [], [[], [], [], []]
+        looked = [[], [], [], []]
         for i in range(GROUP):
             row = cells[i : i + 1]
             hot = lane_onehot(row, lane_count, per_block)
             hits = row_hits(row, row_count, lane_count, per_block)
-            hots.append(hot)
-            hit_list.append(hits)
             both = jnp.dot(
                 table[owner_ref[start + i]], hot, preferred_element_type=jnp.float32
             )
@@ -140,13 +137,7 @@
         mass = SOLID_DENSITY * (math.pi / 6 * diam * diam * diam)
         for comp in range(3):
             accel_ref[comp, pl.ds(start, GROUP), :] = force[comp] / mass
-        adds = []
-        for i in range(GROUP):
-            rows = spread_rows(hit_list[i], [force[comp][i : i + 1] for comp in range(3)])
-            adds.append(onto_cells(rows, hots[i]))
-        for i in range(GROUP):
-            owner = owner_ref[start + i]
-            out_ref[owner] = out_ref[owner] + adds[i]
+            force_ref[comp, pl.ds(start, GROUP), :] = force[comp]
 
 
 def each(first, last, body):
@@ -300,33 +291,31 @@
             (x, p.gy, p.gz),
         )
 
+    def start_one(self, x):
+        p = self.plane
+        p.others_y(lambda y: self.along_y(x, y, p.gy).start())
+
     def start(self):
-        p = self.plane
-
-        def one(x):
-            p.others_y(lambda y: self.along_y(x, y, p.gy).start())
-
-        p.others_x(one)
-        one(p.gx)
+        self.plane.others_x(self.start_one)
+        self.start_one(self.plane.gx)
+
+    def add_one(self, x):
+        p = self.plane
+        self.middle[x] = self.source[p.owner(x, p.gy)]
+
+        def add(y):
+            self.along_y(x, y, y).wait_recv()
+            self.middle[x] = self.middle[x] + self.first[y, x]
+
+        p.others_y(add)
+
+    def forward_one(self, x):
+        self.add_one(x)
+        self.along_x(x, self.plane.gx).start()
 
     def forward(self):
-        p = self.plane
-
-        def one(x):
-            self.middle[x] = self.source[p.owner(x, p.gy)]
-
-            def add(y):
-                self.along_y(x, y, y).wait_recv()
-                self.middle[x] = self.middle[x] + self.first[y, x]
-
-            p.others_y(add)
-
-        def send(x):
-            one(x)
-            self.along_x(x, p.gx).start()
-
-        p.others_x(send)
-        one(p.gx)
+        self.plane.others_x(self.forward_one)
+        self.add_one(self.plane.gx)
 
     def total(self, out_ref):
         p = self.plane
@@ -514,13 +503,59 @@
     solid_gather.finish()
 
 
-def source_kernel(sizes, part_ref, out_ref, *rest):
-    plane = Plane(*sizes)
+def source_kernel(sizes, owner_ref, cell_ref, force_ref, out_ref, part_ref, hot_ref, *rest):
+    size_x, size_y = sizes
+    blocks, per_block = cell_ref.shape
+    lane_count = out_ref.shape[1]
+    row_count = out_ref.shape[0] // 3
+    dense = size_y * row_count
+    shift = lane_count.bit_length() - 1
+    plane = Plane(size_x, size_y)
     barrier = pltpu.get_barrier_semaphore()
-    pl.semaphore_wait(barrier, plane.greet(barrier))
+    greeted = plane.greet(barrier)
+
+    def fill_hot(group):
+        cells = cell_ref[pl.ds(pl.multiple_of(group * GROUP, GROUP), GROUP), :]
+        hots = [lane_onehot(cells[i : i + 1], lane_count, per_block) for i in range(GROUP)]
+        hot_ref[group] = jnp.concatenate(hots, axis=1)
+
+    each(0, blocks // GROUP, fill_hot)
+    part_ref[...] = jnp.zeros_like(part_ref)
+    pl.semaphore_wait(barrier, greeted)
     scatter = Scatter(plane, part_ref, *rest)
-    scatter.start()
-    scatter.forward()
+
+    def deposit(x):
+        def step(group):
+            start = pl.multiple_of(group * GROUP, GROUP)
+            cells = cell_ref[pl.ds(start, GROUP), :]
+            force = [force_ref[comp, pl.ds(start, GROUP), :] for comp in range(3)]
+            ids = lax.broadcasted_iota(jnp.int32, (dense, per_block), 0) + x * dense
+            rows = []
+            for i in range(GROUP):
+                row = lax.shift_right_logical(cells[i : i + 1], shift)
+                hits = ids == owner_ref[start + i] * row_count + row
+                rows.append(spread_rows(hits, [force[comp][i : i + 1] for comp in range(3)]))
+            add = onto_cells(jnp.concatenate(rows, axis=1), hot_ref[group])
+            for y in range(size_y):
+                owner = x * size_y + y
+                for comp in range(3):
+                    into = pl.ds(comp * row_count, row_count)
+                    piece = add[comp * dense + y * row_count :][:row_count]
+                    part_ref[owner, into, :] = part_ref[owner, into, :] + piece
+
+        each(0, blocks // GROUP, step)
+
+    def one_x(r):
+        x = lax.rem(plane.gx + r, size_x)
+        deposit(x)
+        scatter.start_one(x)
+
+        @pl.when(r > 1)
+        def _():
+            scatter.forward_one(lax.rem(plane.gx + r - 1, size_x))
+
+    each(1, size_x + 1, one_x)
+    scatter.add_one(plane.gx)
     scatter.total(out_ref)
     scatter.finish()
 
@@ -575,11 +610,11 @@
         fluid_velocity.reshape(3 * row_count, lane_count),
     )
 
-    accel, force_part, voidage = pl.pallas_call(
+    accel, force, voidage = pl.pallas_call(
         force_kernel,
         out_shape=(
             full(3, *diameter.shape),
-            full(owners, 3 * row_count, lane_count),
+            full(3, *diameter.shape),
             full(row_count, lane_count),
         ),
         in_specs=[smem] + [vmem] * 6,
@@ -592,14 +627,20 @@
     total = pl.pallas_call(
         functools.partial(source_kernel, (size_x, size_y)),
         out_shape=full(3 * row_count, lane_count),
-        in_specs=[vmem],
+        in_specs=[smem] + [vmem] * 2,
         out_specs=vmem,
-        scratch_shapes=scatter_scratch(size_x, size_y, 3 * row_count, lane_count),
+        scratch_shapes=[
+            pltpu.VMEM((owners, 3 * row_count, lane_count), jnp.float32),
+            pltpu.VMEM(
+                (diameter.shape[0] // GROUP, lane_count, GROUP * diameter.shape[1]), jnp.bfloat16
+            ),
+        ]
+        + scatter_scratch(size_x, size_y, 3 * row_count, lane_count),
         compiler_params=pltpu.CompilerParams(
             vmem_limit_bytes=limit, collective_id=1, has_side_effects=True
         ),
         name="sum_source",
-    )(force_part)
+    )(owner_list, particle_cell, force)
     voidage = voidage.reshape(bx, by, lane_count)
     brick = (3, bx, by, lane_count)
     weight = TIME_STEP / (FLUID_DENSITY * voidage)

time: 61.4 us -> 63.4 us (1.033)
  Pallas kernels: 58.1 us -> 60.1 us
    pallas_call x1, Pallas kernels: 16.3 us -> 21.6 us  [per_device(): pl.pallas_call(functools.partial(source_kernel, (size_x, size_y)), out_sh...]
    pallas_call x1, Pallas kernels: 9.31 us -> 5.95 us  [per_device(): pl.pallas_call(force_kernel, out_shape=(full(3, *diameter.shape), full(3,...]
where the time goes in v5:
time: 63.4 us; the launch traced here: 63.1 us
  Pallas kernels  60.1 us (95%)
  other arithmetic  2.32 us (4%)
  between operations  0.66 us (1%)
    pallas_call x1, Pallas kernels, per_device(): pl.pallas_call(functools.partial(gather_kernel, (size_x, size_y, size_z,...  32.5 us
    pallas_call x1, Pallas kernels, per_device(): pl.pallas_call(functools.partial(source_kernel, (size_x, size_y)), out_sh...  21.6 us
    pallas_call x1, Pallas kernels, per_device(): pl.pallas_call(force_kernel, out_shape=(full(3, *diameter.shape), full(3,...  5.95 us
    sub x1, other arithmetic, per_device(): fluid_next = base.reshape(brick) - total.reshape(brick) * weight[None]  1.55 us

profile of v5, /device:TPU:0, one launch (start us, length us, event | category | flops | bytes accessed | tf_op | source)
XLA Modules:
  0.0 63.1 jit_solution(11892819413470740973)
XLA Ops:
  0.6 32.5 %gather_plane.1 = (f32[8,96,256]{2,1,0:T(8,128)}, f32[8,32,256]{2,1,0:T(8,128)}, f32[32,256]{1,0:T(8,128)}, f32[96,256]{1,0:T(8,128)}) custom-call(s32[64]{0:T(128)} %bitcast.13, s32[64,128]{1,0:T(8,128)} %cell_ref.5, f32[64,128]{1,0:T(8,128)} %diam_ref.3, f32[96,256]{1,0:T(8,128)} %bitcast.10), custom_call_target="tpu_custom_call" | custom-call | tf_op jit(solution)/shard_map/gather_plane/pallas_call | solution.py:577
  33.2 5.9 %force_deposit.1 = (f32[3,64,128]{2,1,0:T(8,128)}, f32[3,64,128]{2,1,0:T(8,128)}, f32[32,256]{1,0:T(8,128)}) custom-call(s32[64]{0:T(128)} %bitcast.14, s32[64,128]{1,0:T(8,128)} %cell_ref.5, f32[64,128]{1,0:T(8,128)} %diam_ref.3, f32[3,64,128]{2,1,0:T(8,128)} %bitcast.9, f32[8,96,256]{2,1,0:T(8,128)} %get-tuple-element.10.vel_ref, ...), custom_call_target="tpu_custom_call" | custom-call | tf_op jit(solution)/shard_map/force_deposit/pallas_call | solution.py:613
  39.1 0.8 %multiply_divide_fusion = f32[4,8,256]{2,1,0:T(8,128)S(1)} fusion(f32[32,256]{1,0:T(8,128)} %get-tuple-element.14), kind=kLoop, calls=%fused_computation.1 | loop fusion | flops 16384 | bytes 65536 | tf_op jit(solution)/shard_map/div | solution.py:646
  39.9 0.0 copy-start
  39.9 21.6 %sum_source.1 = f32[96,256]{1,0:T(8,128)} custom-call(s32[64]{0:T(128)} %bitcast.15, s32[64,128]{1,0:T(8,128)} %cell_ref.5, f32[3,64,128]{2,1,0:T(8,128)} %get-tuple-element.16.force_ref), custom_call_target="tpu_custom_call" | custom-call | tf_op jit(solution)/shard_map/sum_source/pallas_call | solution.py:627
  61.5 0.0 copy-done
  61.5 1.5 %multiply_subtract_fusion = f32[3,4,8,256]{3,2,1,0:T(8,128)} fusion(f32[3,4,8,256]{3,2,1,0:T(8,128)S(1)} %bitcast.11, f32[3,4,8,256]{3,2,1,0:T(8,128)} %bitcast.8, f32[4,8,256]{2,1,0:T(8,128)S(1)} %multiply_divide_fusion), kind=kLoop, calls=%fused_computation | loop fusion | flops 49152 | bytes 327680 | tf_op jit(solution)/shard_map/sub | solution.py:647
Async XLA Ops:
  39.9 21.6 %copy-start = (f32[96,256]{1,0:T(8,128)S(1)}, f32[96,256]{1,0:T(8,128)}, u32[]{:S(2)}) copy-start(f32[96,256]{1,0:T(8,128)} %get-tuple-element.15) | copy-start | bytes 294916

commit v6 on v4

--- a/solution.py
+++ b/solution.py
@@ -442,9 +442,8 @@
         copy.start()
     deposit_volume(owner_ref, cell_ref, diam_ref, partial_ref)
     scatter.start()
-    vel.forward(1, size_x - 1)
+    vel.forward(1, size_x)
     scatter.forward()
-    vel.forward(size_x - 1, size_x)
     scatter.total(solid_ref)
     solid = solid_ref[...]
     slot(me)[...] = solid.reshape(bx, by, lane_count)
@@ -523,6 +522,11 @@
     scatter.forward()
     scatter.total(out_ref)
     scatter.finish()
+
+
+def last_kernel(base_ref, total_ref, void_ref, out_ref):
+    weight = TIME_STEP / (FLUID_DENSITY * void_ref[...])
+    out_ref[...] = base_ref[...] - total_ref[...] * weight[None]
 
 
 def per_device(fluid_velocity, particle_velocity, diameter, particle_cell, block_owner):
@@ -602,8 +606,15 @@
     )(force_part)
     voidage = voidage.reshape(bx, by, lane_count)
     brick = (3, bx, by, lane_count)
-    weight = TIME_STEP / (FLUID_DENSITY * voidage)
-    fluid_next = base.reshape(brick) - total.reshape(brick) * weight[None]
+    fluid_next = pl.pallas_call(
+        last_kernel,
+        out_shape=full(3, row_count, lane_count),
+        in_specs=[vmem] * 3,
+        out_specs=vmem,
+        compiler_params=pltpu.CompilerParams(vmem_limit_bytes=limit),
+        name="last_step",
+    )(base.reshape(3, row_count, lane_count), total.reshape(3, row_count, lane_count), void_own)
+    fluid_next = fluid_next.reshape(brick)
     return (
         accel.transpose(1, 0, 2),
         voidage,

time: 61.4 us -> 60.3 us (0.982)
  other arithmetic: 2.32 us -> 0 us
  Pallas kernels: 58.1 us -> 59.4 us
    pallas_call x0 -> x1, Pallas kernels: none -> 1.6 us  [per_device(): pl.pallas_call(last_kernel, out_shape=full(3, row_count, lane_count), in_...]
    sub x1 -> x0, other arithmetic: 1.55 us -> none  [per_device(): fluid_next = base.reshape(brick) - total.reshape(brick) * weight[None]]
    div x1 -> x0, other arithmetic: 0.77 us -> none  [per_device(): weight = TIME_STEP / (FLUID_DENSITY * voidage)]
where the time goes in v6:
time: 60.3 us; the launch traced here: 60 us
  Pallas kernels  59.4 us (99%)
  between operations  0.65 us (1%)
    pallas_call x1, Pallas kernels, per_device(): pl.pallas_call(functools.partial(gather_kernel, (size_x, size_y, size_z,...  32.7 us
    pallas_call x1, Pallas kernels, per_device(): pl.pallas_call(functools.partial(source_kernel, (size_x, size_y)), out_sh...  15.7 us
    pallas_call x1, Pallas kernels, per_device(): pl.pallas_call(force_kernel, out_shape=(full(3, *diameter.shape), full(ow...  9.3 us
    pallas_call x1, Pallas kernels, per_device(): pl.pallas_call(last_kernel, out_shape=full(3, row_count, lane_count), in_...  1.6 us

profile of v6, /device:TPU:0, one launch (start us, length us, event | category | flops | bytes accessed | tf_op | source)
XLA Modules:
  0.0 60.0 jit_solution(13122949530728550049)
XLA Ops:
  0.6 32.7 %gather_plane.1 = (f32[8,96,256]{2,1,0:T(8,128)}, f32[8,32,256]{2,1,0:T(8,128)}, f32[32,256]{1,0:T(8,128)}, f32[96,256]{1,0:T(8,128)}) custom-call(s32[64]{0:T(128)} %bitcast.13, s32[64,128]{1,0:T(8,128)} %cell_ref.3, f32[64,128]{1,0:T(8,128)} %diam_ref.3, f32[96,256]{1,0:T(8,128)} %bitcast.10), custom_call_target="tpu_custom_call" | custom-call | tf_op jit(solution)/shard_map/gather_plane/pallas_call | solution.py:546
  33.4 9.3 %force_deposit.1 = (f32[3,64,128]{2,1,0:T(8,128)}, f32[8,96,256]{2,1,0:T(8,128)}, f32[32,256]{1,0:T(8,128)}) custom-call(s32[64]{0:T(128)} %bitcast.14, s32[64,128]{1,0:T(8,128)} %cell_ref.3, f32[64,128]{1,0:T(8,128)} %diam_ref.3, f32[3,64,128]{2,1,0:T(8,128)} %bitcast.9, f32[8,96,256]{2,1,0:T(8,128)} %get-tuple-element.10.vel_ref, ...), custom_call_target="tpu_custom_call" | custom-call | tf_op jit(solution)/shard_map/force_deposit/pallas_call | solution.py:582
  42.7 15.7 %sum_source.1 = f32[96,256]{1,0:T(8,128)} custom-call(f32[8,96,256]{2,1,0:T(8,128)} %get-tuple-element.16.part_ref), custom_call_target="tpu_custom_call" | custom-call | tf_op jit(solution)/shard_map/sum_source/pallas_call | solution.py:596
  58.4 1.6 %last_step.1 = f32[3,32,256]{2,1,0:T(8,128)} custom-call(f32[3,32,256]{2,1,0:T(8,128)} %bitcast.11, f32[3,32,256]{2,1,0:T(8,128)} %bitcast.8, f32[32,256]{1,0:T(8,128)} %get-tuple-element.12.own_ref.void_ref), custom_call_target="tpu_custom_call" | custom-call | tf_op jit(solution)/shard_map/last_step/pallas_call | solution.py:609
